TPU v7x, 512 devices: a whole 4x8x8 slice. The times are simulated.
512 devices in a mesh: sub: 4 (over y_hi), gy: 4 (over x), gz: 32 (over z, y_lo, core).
Axes of the slice: x: 4, y: 8 (y_hi: 4, y_lo: 2; y = y_hi * 2 + y_lo), z: 8, core: 2. Of those that a mesh axis runs over, the one named last changes fastest.
Arguments:
- source: float32 [4, 4, 512, 4096], P('sub', None, 'gy', 'gz'), may hold values from -6 to 6
- start_field: float32 [4, 4, 512, 4096], P('sub', None, 'gy', 'gz'), may hold values from -6 to 6
- classes: int32 [4, 4, 512, 4096], P('sub', None, 'gy', 'gz'), may hold values from 0 to 7
- class_table: float32 [8], replicated, may hold values from 0.2 to 5
- chain_place: int32 [4], replicated, may hold values from 0 to 3, as said below
- multipliers: float32 [4, 2, 512, 4096], P('sub', None, 'gy', 'gz'), may hold values from -6 to 6
Outputs:
- temperature: float32 [4, 4, 512, 4096], P('sub', None, 'gy', 'gz')
- new_multipliers: float32 [4, 2, 512, 4096], P('sub', None, 'gy', 'gz')
Inputs may be any that keep to these rules, and one draw needn't show every extreme that they name: `chain_place`: each place 0 to 3 occurs once.
All inputs are finite; a program needn't handle non-finite values.
Results may differ from a plain program's by a relative error of at most 0.0003.
Values sent between devices are 32-bit elements; how exact they have to be, the bound alone decides.
A program may use at most 64 MiB of HBM per device.

v0:
```python
import jax
import jax.numpy as jnp
from jax import lax
from jax.sharding import PartitionSpec as P

SWEEPS = 4


ROBIN = 1.0
CAPACITY = 0.5
LOW_BOUND = 0.1
HIGH_BOUND = 2.0


def with_halo(block, sides, width):
    for axis, dim in sides:
        count = lax.axis_size(axis)
        forward = [(i, i + 1) for i in range(count - 1)]
        backward = [(target, source) for source, target in forward]
        low = lax.ppermute(
            lax.slice_in_dim(block, block.shape[dim] - width, None, axis=dim), axis, forward
        )
        high = lax.ppermute(lax.slice_in_dim(block, 0, width, axis=dim), axis, backward)
        block = jnp.concatenate([low, block, high], axis=dim)
    return block


def harmonic(first, second):
    total = first + second
    safe = jnp.where(total > 0.0, total, 1.0)
    return 2.0 * first * second / safe


def conductivity(classes, table):
    total = jnp.zeros(classes.shape, jnp.float32)
    for index in range(table.shape[0]):
        total = total + jnp.where(classes == index, table[index], 0.0)
    return total


def face_terms(cond, cond_pad):
    y_next = harmonic(cond, cond_pad[:, 2:, 1:-1])
    y_prev = harmonic(cond, cond_pad[:, :-2, 1:-1])
    z_next = harmonic(cond, cond_pad[:, 1:-1, 2:])
    z_prev = harmonic(cond, cond_pad[:, 1:-1, :-2])
    x_link = harmonic(cond[1:], cond[:-1])
    return (y_next, y_prev, z_next, z_prev, x_link)


def build_operator(cond, cond_pad, source, mults, has_lower, has_upper):
    extent = cond.shape[0]
    stored = face_terms(cond, cond_pad)
    zero_plane = jnp.zeros_like(cond[:1])
    x_link = stored[4]
    x_sum = jnp.concatenate([x_link, zero_plane], 0) + jnp.concatenate([zero_plane, x_link], 0)
    layer = lax.broadcasted_iota(jnp.int32, cond.shape, 0)
    lower_coef = jnp.where(has_lower, ROBIN, 2.0 * cond[0])
    upper_coef = jnp.where(has_upper, ROBIN, 2.0 * cond[-1])
    diag = CAPACITY + stored[0] + stored[1] + stored[2] + stored[3] + x_sum
    diag = (
        diag
        + jnp.where(layer == 0, lower_coef[None], 0.0)
        + jnp.where(layer == extent - 1, upper_coef[None], 0.0)
    )
    rhs = source + jnp.where(layer == 0, jnp.where(has_lower, mults[0], 0.0)[None], 0.0)
    rhs = rhs + jnp.where(layer == extent - 1, jnp.where(has_upper, mults[1], 0.0)[None], 0.0)

    def apply(field, fpad):
        near = stored[0] * fpad[:, 2:, 1:-1] + stored[1] * fpad[:, :-2, 1:-1]
        near = near + stored[2] * fpad[:, 1:-1, 2:] + stored[3] * fpad[:, 1:-1, :-2]
        near = (
            near
            + jnp.concatenate([stored[4] * field[1:], zero_plane], 0)
            + jnp.concatenate([zero_plane, stored[4] * field[:-1]], 0)
        )
        return diag * field - near

    return (diag, rhs, apply)


def chebyshev(start_field, start_pad, diag, rhs, apply, rim_fn):
    center = (HIGH_BOUND + LOW_BOUND) / 2.0
    half = (HIGH_BOUND - LOW_BOUND) / 2.0
    sigma = center / half
    field = start_field
    resid = rhs - apply(field, start_pad)
    step = resid / (diag * center)
    rho = 1.0 / sigma
    for sweep in range(SWEEPS):
        field = field + step
        if sweep < SWEEPS - 1:
            resid = resid - apply(step, rim_fn(step))
            rho_new = 1.0 / (2.0 * sigma - rho)
            step = rho_new * rho * step + 2.0 * rho_new / half * resid / diag
            rho = rho_new
    return field


def sweep_halo(step):
    return with_halo(step, (("gy", 1), ("gz", 2)), 1)


def shards(source, start_field, classes, class_table, chain_place, multipliers):
    source = source[0]
    start_field = start_field[0]
    classes = classes[0]
    mults = multipliers[0]
    sub_index = lax.axis_index("sub")
    count = lax.axis_size("sub")
    places = jnp.arange(count, dtype=jnp.int32)
    my_place = jnp.sum(jnp.where(places == sub_index, chain_place, 0))
    lower_hit = chain_place == my_place - 1
    upper_hit = chain_place == my_place + 1
    has_lower = jnp.any(lower_hit)
    has_upper = jnp.any(upper_hit)
    cond = conductivity(classes, class_table)
    both = with_halo(jnp.stack([start_field, cond]), (("gy", 2), ("gz", 3)), 1)
    diag, rhs, apply = build_operator(cond, both[1], source, mults, has_lower, has_upper)
    field = chebyshev(start_field, both[0], diag, rhs, apply, sweep_halo)
    lower_pack = 2.0 * ROBIN * field[0] - mults[0]
    upper_pack = 2.0 * ROBIN * field[-1] - mults[1]
    gathered = lax.all_gather(jnp.stack([lower_pack, upper_pack])[None], "sub", axis=0, tiled=True)
    from_lower = jnp.sum(jnp.where(lower_hit[:, None, None], gathered[:, 1], 0.0), 0)
    from_upper = jnp.sum(jnp.where(upper_hit[:, None, None], gathered[:, 0], 0.0), 0)
    new_mults = jnp.stack([from_lower, from_upper])[None]
    return (field[None], new_mults)


def solution(mesh):
    return jax.shard_map(
        shards,
        mesh=mesh,
        in_specs=(
            P("sub", None, "gy", "gz"),
            P("sub", None, "gy", "gz"),
            P("sub", None, "gy", "gz"),
            P(),
            P(),
            P("sub", None, "gy", "gz"),
        ),
        out_specs=(P("sub", None, "gy", "gz"), P("sub", None, "gy", "gz")),
        check_vma=False,
    )
```

profile of v0, /device:TPU:262, one launch (start us, length us, event | category | flops | bytes accessed | tf_op | source)
XLA Modules:
  0.0 122.5 jit_solution(13855226200549805236)
XLA Ops:
  0.6 0.0 copy-start
  0.7 1.6 %fusion.79 = (f32[1]{0:T(128)}, f32[1]{0:T(128)}, f32[1]{0:T(128)}, f32[1]{0:T(128)}, f32[1]{0:T(128)}, /*index=5*/f32[1]{0:T(128)}, f32[1]{0:T(128)}, f32[1]{0:T(128)}) fusion(f32[8]{0:T(128)} %param.9), kind=kLoop, calls=%fused_computation.152 | loop fusion | bytes 64 | tf_op jit(solution)/shard_map/slice | solution.py:37
  2.3 6.3 %add_add_fusion = f32[1,4,128,128]{3,2,1,0:T(8,128)S(1)} fusion(s32[1,4,128,128]{3,2,1,0:T(8,128)} %param.8, f32[]{:T(128)} %bitcast.11, f32[]{:T(128)} %bitcast.10, f32[]{:T(128)} %bitcast.9, f32[]{:T(128)} %bitcast.8, f32[]{:T(128)} %bitcast.7, f32[]{:T(128)} %bitcast.6, f32[]{:T(128)} %bitcast.5, f32[]{:T(128)} %bitcast.4), kind=kLoop, calls=%fused_computation.105 | loop fusion | flops 1507328 | bytes 524320 | tf_op jit(solution)/shard_map/add | solution.py:37
  8.5 0.0 copy-start.3
  8.6 0.8 pad_maximum_fusion.31
  9.3 1.3 %collective-permute-start = (f32[2,4,1,128]{3,2,1,0:T(1,128)S(1)}, f32[2,4,1,128]{3,2,1,0:T(1,128)S(1)}, u32[]{:S(2)}, u32[]{:S(2)}) collective-permute-start(f32[2,4,1,128]{3,2,1,0:T(1,128)S(1)} %get-tuple-element.25), channel_id=1, source_target_pairs={{0,32},{32,64},{64,96},{1,33},{33,65},{65,97},{2,34},{34,66},{66,9... | collective-permute-start | bytes 12296 | tf_op jit(solution)/shard_map/ppermute | solution.py:20
  10.6 4.5 %collective-permute-start.1 = (f32[2,4,1,128]{3,2,1,0:T(1,128)S(1)}, f32[2,4,1,128]{3,2,1,0:T(1,128)S(1)}, u32[]{:S(2)}, u32[]{:S(2)}) collective-permute-start(f32[2,4,1,128]{3,2,1,0:T(1,128)S(1)} %get-tuple-element.26), channel_id=1, source_target_pairs={{32,0},{64,32},{96,64},{33,1},{65,33},{97,65},{34,2},{66,34},{98,6... | collective-permute-start | bytes 12296 | tf_op jit(solution)/shard_map/ppermute | solution.py:23
  15.2 0.1 bitcast_multiply_fusion.3
  15.3 0.7 fusion.62
  17.2 0.7 fusion.70
  17.9 1.2 fusion.61
  19.0 0.0 collective-permute-done
  19.1 0.0 collective-permute-done.1
  19.1 0.1 pad_maximum_fusion.1
  19.1 0.2 fusion.72
  19.3 0.3 copy.50
  19.7 1.9 %collective-permute-start.2 = (f32[2,4,130,1]{2,1,3,0:T(4,128)S(1)}, f32[2,4,130,1]{2,1,3,0:T(4,128)S(1)}, u32[]{:S(2)}, u32[]{:S(2)}) collective-permute-start(f32[2,4,130,1]{2,1,3,0:T(4,128)S(1)} %copy.50), channel_id=1, source_target_pairs={{0,1},{1,2},{2,3},{3,4},{4,5},{5,6},{6,7},{7,8},{8,9},{9,10},{10,1... | collective-permute-start | bytes 12488 | tf_op jit(solution)/shard_map/ppermute | solution.py:20
  21.6 0.3 copy.51
  21.9 5.8 %collective-permute-start.3 = (f32[2,4,130,1]{2,1,3,0:T(4,128)S(1)}, f32[2,4,130,1]{2,1,3,0:T(4,128)S(1)}, u32[]{:S(2)}, u32[]{:S(2)}) collective-permute-start(f32[2,4,130,1]{2,1,3,0:T(4,128)S(1)} %copy.51), channel_id=1, source_target_pairs={{1,0},{2,1},{3,2},{4,3},{5,4},{6,5},{7,6},{8,7},{9,8},{10,9},{11,1... | collective-permute-start | bytes 12488 | tf_op jit(solution)/shard_map/ppermute | solution.py:23
  27.7 0.0 collective-permute-done.2
  27.7 0.2 copy.52
  28.0 1.1 collective-permute-done.3
  29.0 0.2 copy.53
  29.3 0.5 pad_maximum_fusion
  29.8 0.0 copy-start.1
  29.8 0.0 copy-start.4
  29.9 0.1 slice_bitcast_fusion.1
  29.9 0.8 copy-done.1
  30.8 0.1 copy-done.4
  30.9 6.0 %multiply_divide_fusion = (f32[4,128,128]{2,1,0:T(8,128)S(1)}, f32[4,128,128]{2,1,0:T(8,128)S(1)}, f32[4,128,128]{2,1,0:T(8,128)S(1)}, f32[4,128,128]{2,1,0:T(8,...) fusion(f32[3,128,128]{2,1,0:T(8,128)S(1)} %bitcast_multiply_fusion.2, ...), kind=kLoop, calls=%fused_computation.108 | loop fusion | flops 4718592 | bytes 5570600 | tf_op jit(solution)/shard_map/div | solution.py:87
  36.9 2.7 %collective-permute-start.4 = (f32[4,1,128]{2,1,0:T(1,128)S(1)}, f32[4,1,128]{2,1,0:T(1,128)S(1)}, u32[]{:S(2)}, u32[]{:S(2)}) collective-permute-start(f32[4,1,128]{2,1,0:T(1,128)S(1)} %get-tuple-element.46), channel_id=1, source_target_pairs={{32,0},{64,32},{96,64},{33,1},{65,33},{97,65},{34,2},{66,34},{98,6... | collective-permute-start | bytes 6152 | tf_op jit(solution)/shard_map/ppermute | solution.py:23
  39.7 1.3 %collective-permute-start.5 = (f32[4,1,128]{2,1,0:T(1,128)S(1)}, f32[4,1,128]{2,1,0:T(1,128)S(1)}, u32[]{:S(2)}, u32[]{:S(2)}) collective-permute-start(f32[4,1,128]{2,1,0:T(1,128)S(1)} %get-tuple-element.45), channel_id=1, source_target_pairs={{0,32},{32,64},{64,96},{1,33},{33,65},{65,97},{2,34},{34,66},{66,9... | collective-permute-start | bytes 6152 | tf_op jit(solution)/shard_map/ppermute | solution.py:20
  41.0 0.0 collective-permute-done.4
  41.0 4.2 %collective-permute-done.5 = f32[4,1,128]{2,1,0:T(1,128)S(1)} collective-permute-done((f32[4,1,128]{2,1,0:T(1,128)S(1)}, f32[4,1,128]{2,1,0:T(1,128)S(1)}, u32[]{:S(2)}, u32[]{:S(2)}) %collective-permute-start.5) | collective-permute-done | bytes 2080 | tf_op jit(solution)/shard_map/ppermute | solution.py:20
  45.2 0.1 fusion.75
  45.3 4.3 %collective-permute-start.6 = (f32[4,130,1]{2,1,0:T(8,128)S(1)}, f32[4,130,1]{2,1,0:T(8,128)S(1)}, u32[]{:S(2)}, u32[]{:S(2)}) collective-permute-start(f32[4,130,1]{2,1,0:T(8,128)S(1)} %get-tuple-element.39), channel_id=1, source_target_pairs={{1,0},{2,1},{3,2},{4,3},{5,4},{6,5},{7,6},{8,7},{9,8},{10,9},{11,1... | collective-permute-start | bytes 6248 | tf_op jit(solution)/shard_map/ppermute | solution.py:23
  49.6 1.9 %collective-permute-start.7 = (f32[4,130,1]{2,1,0:T(8,128)S(1)}, f32[4,130,1]{2,1,0:T(8,128)S(1)}, u32[]{:S(2)}, u32[]{:S(2)}) collective-permute-start(f32[4,130,1]{2,1,0:T(8,128)S(1)} %get-tuple-element.40), channel_id=1, source_target_pairs={{0,1},{1,2},{2,3},{3,4},{4,5},{5,6},{6,7},{7,8},{8,9},{9,10},{10,1... | collective-permute-start | bytes 6248 | tf_op jit(solution)/shard_map/ppermute | solution.py:20
  51.6 4.4 %collective-permute-done.6 = f32[4,130,1]{2,1,0:T(8,128)S(1)} collective-permute-done((f32[4,130,1]{2,1,0:T(8,128)S(1)}, f32[4,130,1]{2,1,0:T(8,128)S(1)}, u32[]{:S(2)}, u32[]{:S(2)}) %collective-permute-start.6) | collective-permute-done | bytes 2112 | tf_op jit(solution)/shard_map/ppermute | solution.py:23
  56.0 3.6 %collective-permute-done.7 = f32[4,130,1]{2,1,0:T(8,128)S(1)} collective-permute-done((f32[4,130,1]{2,1,0:T(8,128)S(1)}, f32[4,130,1]{2,1,0:T(8,128)S(1)}, u32[]{:S(2)}, u32[]{:S(2)}) %collective-permute-start.7) | collective-permute-done | bytes 2112 | tf_op jit(solution)/shard_map/ppermute | solution.py:20
  59.6 0.4 divide_add_fusion.1
  60.0 2.4 %collective-permute-start.8 = (f32[4,1,128]{2,1,0:T(1,128)S(1)}, f32[4,1,128]{2,1,0:T(1,128)S(1)}, u32[]{:S(2)}, u32[]{:S(2)}) collective-permute-start(f32[4,1,128]{2,1,0:T(1,128)S(1)} %get-tuple-element.44), channel_id=1, source_target_pairs={{32,0},{64,32},{96,64},{33,1},{65,33},{97,65},{34,2},{66,34},{98,6... | collective-permute-start | bytes 6152 | tf_op jit(solution)/shard_map/ppermute | solution.py:23
  62.5 1.3 %collective-permute-start.9 = (f32[4,1,128]{2,1,0:T(1,128)S(1)}, f32[4,1,128]{2,1,0:T(1,128)S(1)}, u32[]{:S(2)}, u32[]{:S(2)}) collective-permute-start(f32[4,1,128]{2,1,0:T(1,128)S(1)} %get-tuple-element.43), channel_id=1, source_target_pairs={{0,32},{32,64},{64,96},{1,33},{33,65},{65,97},{2,34},{34,66},{66,9... | collective-permute-start | bytes 6152 | tf_op jit(solution)/shard_map/ppermute | solution.py:20
  63.8 0.0 collective-permute-done.8
  63.8 4.2 %collective-permute-done.9 = f32[4,1,128]{2,1,0:T(1,128)S(1)} collective-permute-done((f32[4,1,128]{2,1,0:T(1,128)S(1)}, f32[4,1,128]{2,1,0:T(1,128)S(1)}, u32[]{:S(2)}, u32[]{:S(2)}) %collective-permute-start.9) | collective-permute-done | bytes 2080 | tf_op jit(solution)/shard_map/ppermute | solution.py:20
  68.0 0.1 fusion.74
  68.1 1.9 %collective-permute-start.10 = (f32[4,130,1]{2,1,0:T(8,128)S(1)}, f32[4,130,1]{2,1,0:T(8,128)S(1)}, u32[]{:S(2)}, u32[]{:S(2)}) collective-permute-start(f32[4,130,1]{2,1,0:T(8,128)S(1)} %get-tuple-element.37), channel_id=1, source_target_pairs={{1,0},{2,1},{3,2},{4,3},{5,4},{6,5},{7,6},{8,7},{9,8},{10,9},{11,1... | collective-permute-start | bytes 6248 | tf_op jit(solution)/shard_map/ppermute | solution.py:23
  70.0 2.4 %collective-permute-start.11 = (f32[4,130,1]{2,1,0:T(8,128)S(1)}, f32[4,130,1]{2,1,0:T(8,128)S(1)}, u32[]{:S(2)}, u32[]{:S(2)}) collective-permute-start(f32[4,130,1]{2,1,0:T(8,128)S(1)} %get-tuple-element.38), channel_id=1, source_target_pairs={{0,1},{1,2},{2,3},{3,4},{4,5},{5,6},{6,7},{7,8},{8,9},{9,10},{10,1... | collective-permute-start | bytes 6248 | tf_op jit(solution)/shard_map/ppermute | solution.py:20
  72.5 2.8 %collective-permute-done.10 = f32[4,130,1]{2,1,0:T(8,128)S(1)} collective-permute-done((f32[4,130,1]{2,1,0:T(8,128)S(1)}, f32[4,130,1]{2,1,0:T(8,128)S(1)}, u32[]{:S(2)}, u32[]{:S(2)}) %collective-permute-start.10) | collective-permute-done | bytes 2112 | tf_op jit(solution)/shard_map/ppermute | solution.py:23
  75.3 4.8 %collective-permute-done.11 = f32[4,130,1]{2,1,0:T(8,128)S(1)} collective-permute-done((f32[4,130,1]{2,1,0:T(8,128)S(1)}, f32[4,130,1]{2,1,0:T(8,128)S(1)}, u32[]{:S(2)}, u32[]{:S(2)}) %collective-permute-start.11) | collective-permute-done | bytes 2112 | tf_op jit(solution)/shard_map/ppermute | solution.py:20
  80.0 0.4 divide_add_fusion
  80.4 2.2 %collective-permute-start.12 = (f32[4,1,128]{2,1,0:T(1,128)S(1)}, f32[4,1,128]{2,1,0:T(1,128)S(1)}, u32[]{:S(2)}, u32[]{:S(2)}) collective-permute-start(f32[4,1,128]{2,1,0:T(1,128)S(1)} %get-tuple-element.42), channel_id=1, source_target_pairs={{32,0},{64,32},{96,64},{33,1},{65,33},{97,65},{34,2},{66,34},{98,6... | collective-permute-start | bytes 6152 | tf_op jit(solution)/shard_map/ppermute | solution.py:23
  82.6 1.3 %collective-permute-start.13 = (f32[4,1,128]{2,1,0:T(1,128)S(1)}, f32[4,1,128]{2,1,0:T(1,128)S(1)}, u32[]{:S(2)}, u32[]{:S(2)}) collective-permute-start(f32[4,1,128]{2,1,0:T(1,128)S(1)} %get-tuple-element.41), channel_id=1, source_target_pairs={{0,32},{32,64},{64,96},{1,33},{33,65},{65,97},{2,34},{34,66},{66,9... | collective-permute-start | bytes 6152 | tf_op jit(solution)/shard_map/ppermute | solution.py:20
  83.9 0.0 collective-permute-done.12
  83.9 4.2 %collective-permute-done.13 = f32[4,1,128]{2,1,0:T(1,128)S(1)} collective-permute-done((f32[4,1,128]{2,1,0:T(1,128)S(1)}, f32[4,1,128]{2,1,0:T(1,128)S(1)}, u32[]{:S(2)}, u32[]{:S(2)}) %collective-permute-start.13) | collective-permute-done | bytes 2080 | tf_op jit(solution)/shard_map/ppermute | solution.py:20
  88.1 0.1 fusion.73
  88.3 1.9 %collective-permute-start.14 = (f32[4,130,1]{2,1,0:T(8,128)S(1)}, f32[4,130,1]{2,1,0:T(8,128)S(1)}, u32[]{:S(2)}, u32[]{:S(2)}) collective-permute-start(f32[4,130,1]{2,1,0:T(8,128)S(1)} %get-tuple-element.35), channel_id=1, source_target_pairs={{1,0},{2,1},{3,2},{4,3},{5,4},{6,5},{7,6},{8,7},{9,8},{10,9},{11,1... | collective-permute-start | bytes 6248 | tf_op jit(solution)/shard_map/ppermute | solution.py:23
  90.2 2.4 %collective-permute-start.15 = (f32[4,130,1]{2,1,0:T(8,128)S(1)}, f32[4,130,1]{2,1,0:T(8,128)S(1)}, u32[]{:S(2)}, u32[]{:S(2)}) collective-permute-start(f32[4,130,1]{2,1,0:T(8,128)S(1)} %get-tuple-element.36), channel_id=1, source_target_pairs={{0,1},{1,2},{2,3},{3,4},{4,5},{5,6},{6,7},{7,8},{8,9},{9,10},{10,1... | collective-permute-start | bytes 6248 | tf_op jit(solution)/shard_map/ppermute | solution.py:20
  92.7 2.8 %collective-permute-done.14 = f32[4,130,1]{2,1,0:T(8,128)S(1)} collective-permute-done((f32[4,130,1]{2,1,0:T(8,128)S(1)}, f32[4,130,1]{2,1,0:T(8,128)S(1)}, u32[]{:S(2)}, u32[]{:S(2)}) %collective-permute-start.14) | collective-permute-done | bytes 2112 | tf_op jit(solution)/shard_map/ppermute | solution.py:23
  95.4 5.5 %collective-permute-done.15 = f32[4,130,1]{2,1,0:T(8,128)S(1)} collective-permute-done((f32[4,130,1]{2,1,0:T(8,128)S(1)}, f32[4,130,1]{2,1,0:T(8,128)S(1)}, u32[]{:S(2)}, u32[]{:S(2)}) %collective-permute-start.15) | collective-permute-done | bytes 2112 | tf_op jit(solution)/shard_map/ppermute | solution.py:20
  100.9 0.7 fusion.17
  101.6 0.0 copy-start.2
  101.7 20.0 %all-gather = f32[8,128,128]{2,1,0:T(8,128)S(1)} all-gather(f32[2,128,128]{2,1,0:T(8,128)S(1)} %pad_maximum_fusion.29), channel_id=2, replica_groups=mesh['sub'=4,'gy'=4,'gz'=32] {'sub'}, dimensions={0}, use_global_device_ids=true | all-gather | bytes 655360 | tf_op jit(solution)/shard_map/all_gather | solution.py:122
  121.7 0.1 fusion.7
  121.8 0.7 maximum_bitcast_fusion
  (18 shorter events, 0.3 us)
Async XLA Ops:
  0.6 14.6 %copy-start = (f32[1,4,128,128]{3,2,1,0:T(8,128)S(1)}, f32[1,4,128,128]{3,2,1,0:T(8,128)}, u32[]{:S(2)}) copy-start(f32[1,4,128,128]{3,2,1,0:T(8,128)} %param.7) | copy-start | bytes 786436
  0.6 14.6 %copy-start.5 = (s32[4]{0:T(128)S(1)}, s32[4]{0:T(128)}, u32[]{:S(2)}) copy-start(s32[4]{0:T(128)} %param.10) | copy-start | bytes 52
  8.5 9.3 %copy-start.3 = (f32[1,2,128,128]{3,2,1,0:T(8,128)S(1)}, f32[1,2,128,128]{3,2,1,0:T(8,128)}, u32[]{:S(2)}) copy-start(f32[1,2,128,128]{3,2,1,0:T(8,128)} %param.11) | copy-start | bytes 393220
  9.3 9.7 %collective-permute-start = (f32[2,4,1,128]{3,2,1,0:T(1,128)S(1)}, f32[2,4,1,128]{3,2,1,0:T(1,128)S(1)}, u32[]{:S(2)}, u32[]{:S(2)}) collective-permute-start(f32[2,4,1,128]{3,2,1,0:T(1,128)S(1)} %get-tuple-element.25), channel_id=1, source_target_pairs={{0,32},{32,64},{64,96},{1,33},{33,65},{65,97},{2,34},{34,66},{66,9... | collective-permute-start | bytes 12296 | tf_op jit(solution)/shard_map/ppermute | solution.py:20
  10.6 8.4 %collective-permute-start.1 = (f32[2,4,1,128]{3,2,1,0:T(1,128)S(1)}, f32[2,4,1,128]{3,2,1,0:T(1,128)S(1)}, u32[]{:S(2)}, u32[]{:S(2)}) collective-permute-start(f32[2,4,1,128]{3,2,1,0:T(1,128)S(1)} %get-tuple-element.26), channel_id=1, source_target_pairs={{32,0},{64,32},{96,64},{33,1},{65,33},{97,65},{34,2},{66,34},{98,6... | collective-permute-start | bytes 12296 | tf_op jit(solution)/shard_map/ppermute | solution.py:23
  19.7 8.0 %collective-permute-start.2 = (f32[2,4,130,1]{2,1,3,0:T(4,128)S(1)}, f32[2,4,130,1]{2,1,3,0:T(4,128)S(1)}, u32[]{:S(2)}, u32[]{:S(2)}) collective-permute-start(f32[2,4,130,1]{2,1,3,0:T(4,128)S(1)} %copy.50), channel_id=1, source_target_pairs={{0,1},{1,2},{2,3},{3,4},{4,5},{5,6},{6,7},{7,8},{8,9},{9,10},{10,1... | collective-permute-start | bytes 12488 | tf_op jit(solution)/shard_map/ppermute | solution.py:20
  21.9 7.1 %collective-permute-start.3 = (f32[2,4,130,1]{2,1,3,0:T(4,128)S(1)}, f32[2,4,130,1]{2,1,3,0:T(4,128)S(1)}, u32[]{:S(2)}, u32[]{:S(2)}) collective-permute-start(f32[2,4,130,1]{2,1,3,0:T(4,128)S(1)} %copy.51), channel_id=1, source_target_pairs={{1,0},{2,1},{3,2},{4,3},{5,4},{6,5},{7,6},{8,7},{9,8},{10,9},{11,1... | collective-permute-start | bytes 12488 | tf_op jit(solution)/shard_map/ppermute | solution.py:23
  29.8 1.0 copy-start.1
  29.8 1.0 copy-start.4
  36.9 4.0 %collective-permute-start.4 = (f32[4,1,128]{2,1,0:T(1,128)S(1)}, f32[4,1,128]{2,1,0:T(1,128)S(1)}, u32[]{:S(2)}, u32[]{:S(2)}) collective-permute-start(f32[4,1,128]{2,1,0:T(1,128)S(1)} %get-tuple-element.46), channel_id=1, source_target_pairs={{32,0},{64,32},{96,64},{33,1},{65,33},{97,65},{34,2},{66,34},{98,6... | collective-permute-start | bytes 6152 | tf_op jit(solution)/shard_map/ppermute | solution.py:23
  39.7 5.5 %collective-permute-start.5 = (f32[4,1,128]{2,1,0:T(1,128)S(1)}, f32[4,1,128]{2,1,0:T(1,128)S(1)}, u32[]{:S(2)}, u32[]{:S(2)}) collective-permute-start(f32[4,1,128]{2,1,0:T(1,128)S(1)} %get-tuple-element.45), channel_id=1, source_target_pairs={{0,32},{32,64},{64,96},{1,33},{33,65},{65,97},{2,34},{34,66},{66,9... | collective-permute-start | bytes 6152 | tf_op jit(solution)/shard_map/ppermute | solution.py:20
  45.3 10.7 %collective-permute-start.6 = (f32[4,130,1]{2,1,0:T(8,128)S(1)}, f32[4,130,1]{2,1,0:T(8,128)S(1)}, u32[]{:S(2)}, u32[]{:S(2)}) collective-permute-start(f32[4,130,1]{2,1,0:T(8,128)S(1)} %get-tuple-element.39), channel_id=1, source_target_pairs={{1,0},{2,1},{3,2},{4,3},{5,4},{6,5},{7,6},{8,7},{9,8},{10,9},{11,1... | collective-permute-start | bytes 6248 | tf_op jit(solution)/shard_map/ppermute | solution.py:23
  49.6 10.0 %collective-permute-start.7 = (f32[4,130,1]{2,1,0:T(8,128)S(1)}, f32[4,130,1]{2,1,0:T(8,128)S(1)}, u32[]{:S(2)}, u32[]{:S(2)}) collective-permute-start(f32[4,130,1]{2,1,0:T(8,128)S(1)} %get-tuple-element.40), channel_id=1, source_target_pairs={{0,1},{1,2},{2,3},{3,4},{4,5},{5,6},{6,7},{7,8},{8,9},{9,10},{10,1... | collective-permute-start | bytes 6248 | tf_op jit(solution)/shard_map/ppermute | solution.py:20
  60.0 3.7 %collective-permute-start.8 = (f32[4,1,128]{2,1,0:T(1,128)S(1)}, f32[4,1,128]{2,1,0:T(1,128)S(1)}, u32[]{:S(2)}, u32[]{:S(2)}) collective-permute-start(f32[4,1,128]{2,1,0:T(1,128)S(1)} %get-tuple-element.44), channel_id=1, source_target_pairs={{32,0},{64,32},{96,64},{33,1},{65,33},{97,65},{34,2},{66,34},{98,6... | collective-permute-start | bytes 6152 | tf_op jit(solution)/shard_map/ppermute | solution.py:23
  62.5 5.5 %collective-permute-start.9 = (f32[4,1,128]{2,1,0:T(1,128)S(1)}, f32[4,1,128]{2,1,0:T(1,128)S(1)}, u32[]{:S(2)}, u32[]{:S(2)}) collective-permute-start(f32[4,1,128]{2,1,0:T(1,128)S(1)} %get-tuple-element.43), channel_id=1, source_target_pairs={{0,32},{32,64},{64,96},{1,33},{33,65},{65,97},{2,34},{34,66},{66,9... | collective-permute-start | bytes 6152 | tf_op jit(solution)/shard_map/ppermute | solution.py:20
  68.1 7.2 %collective-permute-start.10 = (f32[4,130,1]{2,1,0:T(8,128)S(1)}, f32[4,130,1]{2,1,0:T(8,128)S(1)}, u32[]{:S(2)}, u32[]{:S(2)}) collective-permute-start(f32[4,130,1]{2,1,0:T(8,128)S(1)} %get-tuple-element.37), channel_id=1, source_target_pairs={{1,0},{2,1},{3,2},{4,3},{5,4},{6,5},{7,6},{8,7},{9,8},{10,9},{11,1... | collective-permute-start | bytes 6248 | tf_op jit(solution)/shard_map/ppermute | solution.py:23
  70.0 10.0 %collective-permute-start.11 = (f32[4,130,1]{2,1,0:T(8,128)S(1)}, f32[4,130,1]{2,1,0:T(8,128)S(1)}, u32[]{:S(2)}, u32[]{:S(2)}) collective-permute-start(f32[4,130,1]{2,1,0:T(8,128)S(1)} %get-tuple-element.38), channel_id=1, source_target_pairs={{0,1},{1,2},{2,3},{3,4},{4,5},{5,6},{6,7},{7,8},{8,9},{9,10},{10,1... | collective-permute-start | bytes 6248 | tf_op jit(solution)/shard_map/ppermute | solution.py:20
  80.4 3.5 %collective-permute-start.12 = (f32[4,1,128]{2,1,0:T(1,128)S(1)}, f32[4,1,128]{2,1,0:T(1,128)S(1)}, u32[]{:S(2)}, u32[]{:S(2)}) collective-permute-start(f32[4,1,128]{2,1,0:T(1,128)S(1)} %get-tuple-element.42), channel_id=1, source_target_pairs={{32,0},{64,32},{96,64},{33,1},{65,33},{97,65},{34,2},{66,34},{98,6... | collective-permute-start | bytes 6152 | tf_op jit(solution)/shard_map/ppermute | solution.py:23
  82.6 5.5 %collective-permute-start.13 = (f32[4,1,128]{2,1,0:T(1,128)S(1)}, f32[4,1,128]{2,1,0:T(1,128)S(1)}, u32[]{:S(2)}, u32[]{:S(2)}) collective-permute-start(f32[4,1,128]{2,1,0:T(1,128)S(1)} %get-tuple-element.41), channel_id=1, source_target_pairs={{0,32},{32,64},{64,96},{1,33},{33,65},{65,97},{2,34},{34,66},{66,9... | collective-permute-start | bytes 6152 | tf_op jit(solution)/shard_map/ppermute | solution.py:20
  88.3 7.2 %collective-permute-start.14 = (f32[4,130,1]{2,1,0:T(8,128)S(1)}, f32[4,130,1]{2,1,0:T(8,128)S(1)}, u32[]{:S(2)}, u32[]{:S(2)}) collective-permute-start(f32[4,130,1]{2,1,0:T(8,128)S(1)} %get-tuple-element.35), channel_id=1, source_target_pairs={{1,0},{2,1},{3,2},{4,3},{5,4},{6,5},{7,6},{8,7},{9,8},{10,9},{11,1... | collective-permute-start | bytes 6248 | tf_op jit(solution)/shard_map/ppermute | solution.py:23
  90.2 10.7 %collective-permute-start.15 = (f32[4,130,1]{2,1,0:T(8,128)S(1)}, f32[4,130,1]{2,1,0:T(8,128)S(1)}, u32[]{:S(2)}, u32[]{:S(2)}) collective-permute-start(f32[4,130,1]{2,1,0:T(8,128)S(1)} %get-tuple-element.36), channel_id=1, source_target_pairs={{0,1},{1,2},{2,3},{3,4},{4,5},{5,6},{6,7},{7,8},{8,9},{9,10},{10,1... | collective-permute-start | bytes 6248 | tf_op jit(solution)/shard_map/ppermute | solution.py:20
  101.6 20.8 %copy-start.2 = (f32[4,128,128]{2,1,0:T(8,128)}, f32[4,128,128]{2,1,0:T(8,128)S(1)}, u32[]{:S(2)}) copy-start(f32[4,128,128]{2,1,0:T(8,128)S(1)} %fusion.17) | copy-start | bytes 786436
where the time goes:
time: 123 us; the launch traced here: 122 us
  starting transfers between devices  39.6 us (32%)
  waiting for transfers between devices  37.3 us (30%)
  blocking collectives  20 us (16%)
  other arithmetic  18.8 us (15%)
  local copies, waits for them, and re-layouts  4.45 us (4%)
  between operations  2.27 us (2%)
    ppermute x8, waiting for transfers between devices, with_halo(): lax.ppermute(lax.slice_in_dim(block, block.shape[dim] - width, None, axis...  26.3 us
    ppermute x8, starting transfers between devices, with_halo(): lax.ppermute(lax.slice_in_dim(block, 0, width, axis=dim), axis, backward)  25.8 us
    all_gather x1, blocking collectives, shards(): lax.all_gather(jnp.stack([lower_pack, upper_pack])[None], 'sub', axis=0,...  20 us
    ppermute x8, starting transfers between devices, with_halo(): lax.ppermute(lax.slice_in_dim(block, block.shape[dim] - width, None, axis...  13.8 us
    ppermute x8, waiting for transfers between devices, with_halo(): lax.ppermute(lax.slice_in_dim(block, 0, width, axis=dim), axis, backward)  11 us
    add x1, other arithmetic, conductivity(): total = total + jnp.where(classes == index, table[index], 0.0)  6.26 us
    div x1, other arithmetic, chebyshev(): step = resid / (diag * center)  6.04 us
  transfers between devices with their start and end apart: 16, of which 10 were waited for; matrix products, arithmetic and copies ran while one was open for 3% of the time, Pallas kernels for 0%

commit v1 on v0

v1 whole, which is shorter than its diff:
```python
import jax
import jax.numpy as jnp
from jax import lax
from jax.experimental import pallas as pl
from jax.experimental.pallas import tpu as pltpu
from jax.sharding import PartitionSpec as P

SWEEPS = 4
ROBIN = 1.0
CAPACITY = 0.5
LOW_BOUND = 0.1
HIGH_BOUND = 2.0
MESH = pl.DeviceIdType.MESH

CX = 4
N = 128
TOP = 16
BOTTOM = TOP + N
ROWS = BOTTOM + 16
CHUNKS = ((8, 48), (56, 48), (104, 48))
DIRECTIONS = tuple((dy, dz) for dy in (-1, 0, 1) for dz in (-1, 0, 1) if dy or dz)


def inverse(x):
    guess = pl.reciprocal(x, approx=True)
    return guess * (2.0 - x * guess)


def lookup(classes, splats):
    bit0 = (classes & 1) == 1
    bit1 = (classes & 2) == 2
    bit2 = classes >= 4
    pairs = [jnp.where(bit0, splats[i + 1], splats[i]) for i in range(0, 8, 2)]
    quads = [jnp.where(bit1, pairs[i + 1], pairs[i]) for i in (0, 2)]
    return jnp.where(bit2, quads[1], quads[0])


def kernel(
    source, start, classes, table, chain, mults, t_out, m_out,
    xs, cl, sr, mu, res, hl, hr, pk, hres,
    yn, yp, zn, zp, xn, xp, hyn, hyp, hzn, hzp, hxn, hxp,
    va, vb, hva, hvb, qq, hq, ff, sb, rb,
    load_sem, send_sem, recv_sem, psend, precv,
):
    s = lax.axis_index("sub")
    gy = lax.axis_index("gy")
    gz = lax.axis_index("gz")
    ny = lax.axis_size("gy")
    nz = lax.axis_size("gz")
    subs = lax.axis_size("sub")
    has = {-1: gy > 0, 1: gy < ny - 1}
    hasz = {-1: gz > 0, 1: gz < nz - 1}

    def there(dy, dz):
        ok = None
        for flag in ([has[dy]] if dy else []) + ([hasz[dz]] if dz else []):
            ok = flag if ok is None else jnp.logical_and(ok, flag)
        return ok

    loads = [
        pltpu.make_async_copy(src.at[0], dst.at[:, pl.ds(TOP, N)], load_sem.at[i])
        for i, (src, dst) in enumerate(((start, xs), (classes, cl), (source, sr), (mults, mu)))
    ]
    for copy in loads:
        copy.start()

    barrier = pltpu.get_barrier_semaphore()
    greeted = jnp.int32(subs - 1)
    for dy, dz in DIRECTIONS:
        ok = there(dy, dz)
        greeted = greeted + jnp.where(ok, 1, 0)

        @pl.when(ok)
        def _(dy=dy, dz=dz):
            pl.semaphore_signal(barrier, inc=1, device_id=(s, gy + dy, gz + dz), device_id_type=MESH)

    others = [lax.rem(s + d, subs) for d in range(1, 4)]
    for other in others:
        pl.semaphore_signal(barrier, inc=1, device_id=(other, gy, gz), device_id_type=MESH)

    my_place = chain[s]
    lower = jnp.float32(0.0)
    upper = jnp.float32(0.0)
    for t in range(4):
        lower = lower + jnp.where(chain[t] == my_place - 1, 1.0, 0.0)
        upper = upper + jnp.where(chain[t] == my_place + 1, 1.0, 0.0)

    splats = [jnp.full((8, N), table[i], jnp.float32) for i in range(8)]
    splats = [(0.5 * inverse(v))[:1] for v in splats]

    ones8 = jnp.ones((8, N), jnp.float32)
    for dy, at in ((-1, 8), (1, BOTTOM)):

        @pl.when(jnp.logical_not(has[dy]))
        def _(at=at):
            for l in range(CX):
                xs[l, pl.ds(at, 8)] = ones8
                cl[l, pl.ds(at, 8)] = jnp.ones((8, N), jnp.int32)
                sr[l, pl.ds(at, 8)] = ones8
            for l in range(2):
                mu[l, pl.ds(at, 8)] = ones8
            hl[pl.ds(at, 8)] = ones8
            hr[pl.ds(at, 8)] = ones8

    for dz, ref in ((-1, hl), (1, hr)):

        @pl.when(jnp.logical_not(hasz[dz]))
        def _(ref=ref):
            ref[...] = jnp.ones((ROWS, N), jnp.float32)

    for ref in (va, vb):
        for l in range(CX):
            ref[l, pl.ds(0, 8)] = jnp.zeros((8, N), jnp.float32)
            ref[l, pl.ds(ROWS - 8, 8)] = jnp.zeros((8, N), jnp.float32)
    for ref in (hva, hvb):
        ref[pl.ds(0, 8)] = jnp.zeros((8, N), jnp.float32)
        ref[pl.ds(ROWS - 8, 8)] = jnp.zeros((8, N), jnp.float32)
    for l in range(CX):
        xs[l, pl.ds(0, 8)] = ones8
        xs[l, pl.ds(ROWS - 8, 8)] = ones8
        res[l, pl.ds(0, 8)] = ones8
        res[l, pl.ds(ROWS - 8, 8)] = ones8
    hres[pl.ds(0, 8)] = ones8
    hres[pl.ds(ROWS - 8, 8)] = ones8

    for copy in loads:
        copy.wait()

    lane = lax.broadcasted_iota(jnp.int32, (N, N), 1)
    packed = jnp.zeros((N, N), jnp.float32)
    packed_class = jnp.zeros((N, N), jnp.int32)
    for l in range(CX):
        rhs = sr[l, pl.ds(TOP, N)]
        if l == 0:
            rhs = rhs + lower * mu[0, pl.ds(TOP, N)]
        if l == CX - 1:
            rhs = rhs + upper * mu[1, pl.ds(TOP, N)]
        packed = jnp.where(lane // 8 == l, pltpu.roll(xs[l, pl.ds(TOP, N)], 8 * l + 4, 1), packed)
        packed_class = jnp.where(
            lane // 8 == 4 + l, pltpu.roll(cl[l, pl.ds(TOP, N)], 32 + 8 * l + 4, 1), packed_class
        )
        packed = jnp.where(lane // 8 == 8 + l, pltpu.roll(rhs, 64 + 8 * l + 4, 1), packed)
    pk[...] = jnp.where(lane // 32 == 1, lookup(packed_class, splats), packed)

    pl.semaphore_wait(barrier, greeted)

    sent = []
    k = 0
    for dy, dz in DIRECTIONS:
        own = {-1: 0, 0: 0, 1: N - 8}[dy]
        far = {-1: BOTTOM, 0: TOP, 1: 8}[dy]
        size = N if dy == 0 else 8
        pairs = []
        if dz:
            dst = {-1: hr, 1: hl}[dz]
            pairs.append((pk.at[pl.ds(own, size)], dst.at[pl.ds(far, size)]))
        else:
            for src, dst in ((start, xs), (classes, cl), (source, sr), (mults, mu)):
                pairs.append((src.at[0, :, pl.ds(own, 8)], dst.at[:, pl.ds(far, 8)]))
        for src, dst in pairs:
            copy = pltpu.make_async_remote_copy(
                src_ref=src, dst_ref=dst, send_sem=send_sem.at[k], recv_sem=recv_sem.at[k],
                device_id=(s, gy + dy, gz + dz), device_id_type=MESH,
            )
            pl.when(there(dy, dz))(copy.start)
            sent.append((copy, dy, dz))
            k += 1

    for l in range(CX):
        for r in range(TOP, BOTTOM, 32):
            res[l, pl.ds(r, 32)] = lookup(cl[l, pl.ds(r, 32)], splats)

    for copy, dy, dz in sent:
        pl.when(there(-dy, -dz))(copy.wait_recv)

    for l in range(CX):
        for r in (8, BOTTOM):
            res[l, pl.ds(r, 8)] = lookup(cl[l, pl.ds(r, 8)], splats)

    lane = lax.broadcasted_iota(jnp.int32, (48, N), 1)
    group = lane // 8
    place = lane % 8
    first_lane = lane == 0
    last_lane = lane == N - 1

    def beside(vs, hv):
        edge = None
        nexts, prevs = [], []
        for l in range(CX):
            turned = pltpu.roll(vs[l], 8 * l + 4, 1)
            edge = turned if edge is None else jnp.where(group == l, turned, edge)
            outer = pltpu.roll(hv, N - (8 * l + 4), 1)
            nexts.append(pltpu.roll(jnp.where(first_lane, outer, vs[l]), N - 1, 1))
            prevs.append(pltpu.roll(jnp.where(last_lane, outer, vs[l]), 1, 1))
        hnext = pltpu.roll(jnp.where(place == 4, edge, hv), N - 1, 1)
        hprev = pltpu.roll(jnp.where(place == 3, edge, hv), 1, 1)
        return nexts, prevs, hnext, hprev

    def halo_tile(r, n):
        return jnp.where(place < 4, hl[pl.ds(r, n)], hr[pl.ds(r, n)])

    for r, n in CHUNKS:
        h = halo_tile(r, n)
        hres[pl.ds(r, n)] = jnp.where(lane < 32, pltpu.roll(h, 96, 1), 1.0)
        hva[pl.ds(r, n)] = jnp.where(lane < 32, h, 0.0)

    keep_top = jnp.where(has[-1], 1.0, 0.0)
    keep_bottom = jnp.where(has[1], 1.0, 0.0)
    keep_left = jnp.where(hasz[-1], 1.0, 0.0)
    keep_right = jnp.where(hasz[1], 1.0, 0.0)

    for r, n in CHUNKS:
        row = lax.broadcasted_iota(jnp.int32, (n, N), 0) + r
        rc = [res[l, pl.ds(r, n)] for l in range(CX)]
        hc = hres[pl.ds(r, n)]
        nexts, prevs, hnext, hprev = beside(rc, hc)
        links = [inverse(rc[l] + rc[l + 1]) for l in range(CX - 1)]
        mask_dn = jnp.where(row == BOTTOM - 1, keep_bottom, 1.0)
        mask_up = jnp.where(row == TOP, keep_top, 1.0)
        mask_next = jnp.where(last_lane, keep_right, 1.0)
        mask_prev = jnp.where(first_lane, keep_left, 1.0)
        for l in range(CX):
            a = inverse(rc[l] + res[l, pl.ds(r + 1, n)]) * mask_dn
            b = inverse(rc[l] + res[l, pl.ds(r - 1, n)]) * mask_up
            c = inverse(rc[l] + nexts[l]) * mask_next
            d = inverse(rc[l] + prevs[l]) * mask_prev
            total = CAPACITY + a + b + c + d
            if l > 0:
                total = total + links[l - 1]
            else:
                total = total + (lower * ROBIN + (1.0 - lower) * inverse(rc[l]))
            if l < CX - 1:
                total = total + links[l]
            else:
                total = total + (upper * ROBIN + (1.0 - upper) * inverse(rc[l]))
            e = inverse(total)
            yn[l, pl.ds(r, n)] = a * e
            yp[l, pl.ds(r, n)] = b * e
            zn[l, pl.ds(r, n)] = c * e
            zp[l, pl.ds(r, n)] = d * e
            if l > 0:
                xp[l, pl.ds(r, n)] = links[l - 1] * e
            if l < CX - 1:
                xn[l, pl.ds(r, n)] = links[l] * e
            rhs = sr[l, pl.ds(r, n)]
            if l == 0:
                rhs = rhs + lower * mu[0, pl.ds(r, n)]
            if l == CX - 1:
                rhs = rhs + upper * mu[1, pl.ds(r, n)]
            qq[l, pl.ds(r, n)] = rhs * e
        a = inverse(hc + hres[pl.ds(r + 1, n)]) * mask_dn
        b = inverse(hc + hres[pl.ds(r - 1, n)]) * mask_up
        c = inverse(hc + hnext)
        d = inverse(hc + hprev)
        f = jnp.where(group < CX - 1, inverse(hc + pltpu.roll(hc, N - 8, 1)), 0.0)
        g = jnp.where((group > 0) & (group < CX), inverse(hc + pltpu.roll(hc, 8, 1)), 0.0)
        ends = inverse(hc)
        total = CAPACITY + a + b + c + d + f + g
        total = total + jnp.where(group == 0, lower * ROBIN + (1.0 - lower) * ends, 0.0)
        total = total + jnp.where(group == CX - 1, upper * ROBIN + (1.0 - upper) * ends, 0.0)
        e = inverse(total)
        hyn[pl.ds(r, n)] = a * e
        hyp[pl.ds(r, n)] = b * e
        hzn[pl.ds(r, n)] = c * e
        hzp[pl.ds(r, n)] = d * e
        hxn[pl.ds(r, n)] = f * e
        hxp[pl.ds(r, n)] = g * e
        hq[pl.ds(r, n)] = jnp.where(lane < 32, pltpu.roll(halo_tile(r, n), 64, 1), 0.0) * e

    center = (HIGH_BOUND + LOW_BOUND) / 2.0
    half = (HIGH_BOUND - LOW_BOUND) / 2.0
    sigma = center / half
    rho = 1.0 / sigma
    sends = []
    for sweep in range(SWEEPS):
        if sweep == 0:
            old, hold, new, hnew = xs, hva, va, hvb
            keep, gain = 0.0, 1.0 / center
        else:
            rho_new = 1.0 / (2.0 * sigma - rho)
            keep, gain = rho_new * rho, 2.0 * rho_new / half
            rho = rho_new
            old, hold, new, hnew = ((va, hvb, vb, hva), (vb, hva, va, hvb))[(sweep - 1) % 2]
        last = sweep == SWEEPS - 1
        for part, (r, n) in enumerate(CHUNKS):
            vs = [old[l, pl.ds(r, n)] for l in range(CX)]
            hv = hold[pl.ds(r, n)]
            nexts, prevs, hnext, hprev = beside(vs, hv)
            ends = []
            for l in range(CX):
                near = yn[l, pl.ds(r, n)] * old[l, pl.ds(r + 1, n)]
                near = near + yp[l, pl.ds(r, n)] * old[l, pl.ds(r - 1, n)]
                near = near + zn[l, pl.ds(r, n)] * nexts[l] + zp[l, pl.ds(r, n)] * prevs[l]
                if l > 0:
                    near = near + xp[l, pl.ds(r, n)] * vs[l - 1]
                if l < CX - 1:
                    near = near + xn[l, pl.ds(r, n)] * vs[l + 1]
                q = qq[l, pl.ds(r, n)] - vs[l] + near
                if sweep == 0:
                    step = gain * q
                    field = vs[l] + step
                else:
                    step = keep * vs[l] + gain * q
                    field = ff[l, pl.ds(r, n)] + step
                if last:
                    lo, hi = max(r, TOP), min(r + n, BOTTOM)
                    inner = field[lo - r : hi - r]
                    t_out[0, l, pl.ds(lo - TOP, hi - lo)] = inner
                    if l == 0:
                        ends.append(2.0 * ROBIN * inner - mu[0, pl.ds(lo, hi - lo)])
                    if l == CX - 1:
                        ends.append(2.0 * ROBIN * inner - mu[1, pl.ds(lo, hi - lo)])
                else:
                    qq[l, pl.ds(r, n)] = q
                    new[l, pl.ds(r, n)] = step
                    ff[l, pl.ds(r, n)] = field
            if last:
                for j in (1, 0, 2):
                    above = jnp.where(chain[others[j]] == my_place + 1, 1.0, 0.0)
                    sb[j, pl.ds(lo - TOP, hi - lo)] = above * ends[1] + (1.0 - above) * ends[0]
                    copy = pltpu.make_async_remote_copy(
                        src_ref=sb.at[j, pl.ds(lo - TOP, hi - lo)],
                        dst_ref=rb.at[j, pl.ds(lo - TOP, hi - lo)],
                        send_sem=psend.at[3 * part + j], recv_sem=precv.at[3 * part + j],
                        device_id=(others[j], gy, gz), device_id_type=MESH,
                    )
                    copy.start()
                    sends.append(copy)
            else:
                near = hyn[pl.ds(r, n)] * hold[pl.ds(r + 1, n)] + hyp[pl.ds(r, n)] * hold[pl.ds(r - 1, n)]
                near = near + hzn[pl.ds(r, n)] * hnext + hzp[pl.ds(r, n)] * hprev
                near = near + hxn[pl.ds(r, n)] * pltpu.roll(hv, N - 8, 1) + hxp[pl.ds(r, n)] * pltpu.roll(hv, 8, 1)
                q = hq[pl.ds(r, n)] - hv + near
                hq[pl.ds(r, n)] = q
                hnew[pl.ds(r, n)] = gain * q if sweep == 0 else keep * hv + gain * q

    for copy, dy, dz in sent:
        pl.when(there(dy, dz))(copy.wait_send)
    for copy in sends:
        copy.wait_recv()
    for side, shift in ((0, -1), (1, 1)):
        total = None
        for j in range(3):
            giver = lax.rem(s + subs - (j + 1), subs)
            mine = jnp.where(chain[giver] == my_place + shift, 1.0, 0.0) * rb[j]
            total = mine if total is None else total + mine
        m_out[0, side] = total
    for copy in sends:
        copy.wait_send()


def shards(source, start_field, classes, class_table, chain_place, multipliers):
    wide = pltpu.VMEM((CX, ROWS, N), jnp.float32)
    tall = pltpu.VMEM((ROWS, N), jnp.float32)
    anywhere = pl.BlockSpec(memory_space=pl.ANY)
    scalars = pl.BlockSpec(memory_space=pltpu.SMEM)
    inside = pl.BlockSpec(memory_space=pltpu.VMEM)
    return pl.pallas_call(
        kernel,
        out_shape=(
            jax.ShapeDtypeStruct((1, CX, N, N), jnp.float32),
            jax.ShapeDtypeStruct((1, 2, N, N), jnp.float32),
        ),
        in_specs=[anywhere, anywhere, anywhere, scalars, scalars, anywhere],
        out_specs=(inside, inside),
        scratch_shapes=[
            wide, pltpu.VMEM((CX, ROWS, N), jnp.int32), wide, pltpu.VMEM((2, ROWS, N), jnp.float32),
            wide, tall, tall, pltpu.VMEM((N, N), jnp.float32), tall,
            wide, wide, wide, wide, wide, wide, tall, tall, tall, tall, tall, tall,
            wide, wide, tall, tall, wide, tall, wide,
            pltpu.VMEM((3, N, N), jnp.float32), pltpu.VMEM((3, N, N), jnp.float32),
            pltpu.SemaphoreType.DMA((4,)), pltpu.SemaphoreType.DMA((14,)), pltpu.SemaphoreType.DMA((14,)),
            pltpu.SemaphoreType.DMA((9,)), pltpu.SemaphoreType.DMA((9,)),
        ],
        compiler_params=pltpu.CompilerParams(
            collective_id=0, has_side_effects=True, vmem_limit_bytes=32 * 1024 * 1024
        ),
    )(source, start_field, classes, class_table, chain_place, multipliers)


def solution(mesh):
    blocks = P("sub", None, "gy", "gz")
    return jax.shard_map(
        shards,
        mesh=mesh,
        in_specs=(blocks, blocks, blocks, P(), P(), blocks),
        out_specs=(blocks, blocks),
        check_vma=False,
    )
```

time: 123 us -> 33 us (0.27)
  the two profiles are of different devices: /device:TPU:262 before, /device:TPU:2 now
where the time goes in v1:
time: 33 us; the launch traced here: 32.7 us
  Pallas kernels  25.7 us (78%)
  local copies, waits for them, and re-layouts  6.42 us (19%)
  between operations  0.65 us (2%)
    pallas_call x1, Pallas kernels, shards(): pl.pallas_call(kernel, out_shape=(jax.ShapeDtypeStruct((1, CX, N, N), jnp...  25.7 us
    unnamed x14, local copies, waits for them, and re-layouts  6.42 us

profile of v1, /device:TPU:2, one launch (start us, length us, event | category | flops | bytes accessed | tf_op | source)
XLA Modules:
  0.0 32.7 jit_solution(13375702054761528826)
XLA Ops:
  0.6 0.0 copy-start
  0.6 0.9 %copy-done = f32[1,4,128,128]{3,2,1,0:T(8,128)S(1)} copy-done((f32[1,4,128,128]{3,2,1,0:T(8,128)S(1)}, f32[1,4,128,128]{3,2,1,0:T(8,128)}, u32[]{:S(2)}) %copy-start) | copy-done | bytes 262168
  1.6 0.0 copy-start.1
  1.6 0.9 %copy-done.1 = f32[1,4,128,128]{3,2,1,0:T(8,128)S(1)} copy-done((f32[1,4,128,128]{3,2,1,0:T(8,128)S(1)}, f32[1,4,128,128]{3,2,1,0:T(8,128)}, u32[]{:S(2)}) %copy-start.1) | copy-done | bytes 262168
  2.5 0.0 copy-start.2
  2.5 0.9 %copy-done.2 = s32[1,4,128,128]{3,2,1,0:T(8,128)S(1)} copy-done((s32[1,4,128,128]{3,2,1,0:T(8,128)S(1)}, s32[1,4,128,128]{3,2,1,0:T(8,128)}, u32[]{:S(2)}) %copy-start.2) | copy-done | bytes 262168
  3.5 0.0 copy-start.3
  3.5 0.9 %copy-done.3 = f32[1,2,128,128]{3,2,1,0:T(8,128)S(1)} copy-done((f32[1,2,128,128]{3,2,1,0:T(8,128)S(1)}, f32[1,2,128,128]{3,2,1,0:T(8,128)}, u32[]{:S(2)}) %copy-start.3) | copy-done | bytes 131096
  4.4 0.0 copy-start.4
  4.4 0.7 %copy-done.4 = f32[8]{0:T(128)S(1)} copy-done((f32[8]{0:T(128)S(1)}, f32[8]{0:T(128)}, u32[]{:S(2)}) %copy-start.4) | copy-done | bytes 56
  5.0 0.0 copy-start.5
  5.0 0.7 %copy-done.5 = s32[4]{0:T(128)S(1)} copy-done((s32[4]{0:T(128)S(1)}, s32[4]{0:T(128)}, u32[]{:S(2)}) %copy-start.5) | copy-done | bytes 40
  5.7 25.7 %shard_map.77 = (f32[1,4,128,128]{3,2,1,0:T(8,128)S(1)}, f32[1,2,128,128]{3,2,1,0:T(8,128)S(1)}) custom-call(f32[1,4,128,128]{3,2,1,0:T(8,128)S(1)} %copy-done, f32[1,4,128,128]{3,2,1,0:T(8,128)S(1)} %copy-done.1, s32[1,4,128,128]{3,2,1,0:T(8,128)S(1)} %copy-done.2, f32[8]{0:T(128)S(1)} %copy-done.4, s32[4]{0:T(128)S(1)} %copy-done.5, ...), custom_call_target="tpu_custom_call" | custom-call | tf_op jit(solution)/shard_map/pallas_call | solution.py:358
  31.4 0.7 %copy.10 = f32[1,4,128,128]{3,2,1,0:T(8,128)} copy(f32[1,4,128,128]{3,2,1,0:T(8,128)S(1)} %get-tuple-element.4) | data formatting | bytes 524288
  32.1 0.7 %copy.11 = f32[1,2,128,128]{3,2,1,0:T(8,128)} copy(f32[1,2,128,128]{3,2,1,0:T(8,128)S(1)} %get-tuple-element.5) | data formatting | bytes 262144
Async XLA Ops:
  0.6 1.0 %copy-start = (f32[1,4,128,128]{3,2,1,0:T(8,128)S(1)}, f32[1,4,128,128]{3,2,1,0:T(8,128)}, u32[]{:S(2)}) copy-start(f32[1,4,128,128]{3,2,1,0:T(8,128)} %source.1) | copy-start | bytes 786436
  1.6 0.9 %copy-start.1 = (f32[1,4,128,128]{3,2,1,0:T(8,128)S(1)}, f32[1,4,128,128]{3,2,1,0:T(8,128)}, u32[]{:S(2)}) copy-start(f32[1,4,128,128]{3,2,1,0:T(8,128)} %start.1) | copy-start | bytes 786436
  2.5 0.9 %copy-start.2 = (s32[1,4,128,128]{3,2,1,0:T(8,128)S(1)}, s32[1,4,128,128]{3,2,1,0:T(8,128)}, u32[]{:S(2)}) copy-start(s32[1,4,128,128]{3,2,1,0:T(8,128)} %classes.1) | copy-start | bytes 786436
  3.5 0.9 %copy-start.3 = (f32[1,2,128,128]{3,2,1,0:T(8,128)S(1)}, f32[1,2,128,128]{3,2,1,0:T(8,128)}, u32[]{:S(2)}) copy-start(f32[1,2,128,128]{3,2,1,0:T(8,128)} %mults.1) | copy-start | bytes 393220
  4.4 0.7 %copy-start.4 = (f32[8]{0:T(128)S(1)}, f32[8]{0:T(128)}, u32[]{:S(2)}) copy-start(f32[8]{0:T(128)} %table.1) | copy-start | bytes 100
  5.0 0.7 %copy-start.5 = (s32[4]{0:T(128)S(1)}, s32[4]{0:T(128)}, u32[]{:S(2)}) copy-start(s32[4]{0:T(128)} %chain.1) | copy-start | bytes 52

commit v2 on v0

v2 whole, which is shorter than its diff:
```python
import jax
import jax.numpy as jnp
from jax import lax
from jax.experimental import pallas as pl
from jax.experimental.pallas import tpu as pltpu
from jax.sharding import PartitionSpec as P

SWEEPS = 4
ROBIN = 1.0
CAPACITY = 0.5
LOW_BOUND = 0.1
HIGH_BOUND = 2.0
MESH = pl.DeviceIdType.MESH

CX = 4
N = 128
TOP = 16
BOTTOM = TOP + N
ROWS = BOTTOM + 16
FIRST, COUNT = 8, N + 16
PLANES = 12
DIRECTIONS = ((-1, -1), (-1, 1), (1, -1), (1, 1), (0, 1), (0, -1), (-1, 0), (1, 0))


def inverse(x):
    return pltpu.reciprocal(x, approx=True)


def lookup(classes, splats):
    bit0 = (classes & 1) == 1
    bit1 = (classes & 2) == 2
    bit2 = classes >= 4
    pairs = [jnp.where(bit0, splats[i + 1], splats[i]) for i in range(0, 8, 2)]
    quads = [jnp.where(bit1, pairs[i + 1], pairs[i]) for i in (0, 2)]
    return jnp.where(bit2, quads[1], quads[0])


def lanes(n):
    return lax.broadcasted_iota(jnp.int32, (n, N), 1)


def edge_columns(vs):
    group = lanes(vs[0].shape[0]) // 8
    out = None
    for l in range(CX):
        turned = pltpu.roll(vs[l], 8 * l + 4, 1)
        out = turned if out is None else jnp.where(group == l, turned, out)
    return out


def swapped(edge):
    place = lanes(edge.shape[0]) % 8
    return jnp.where(place == 3, pltpu.roll(edge, N - 1, 1), pltpu.roll(edge, 1, 1))


def kernel(
    source, start, classes, table_hbm, chain_hbm, mults, t_out, m_out,
    table, chain, xs, cl, rh, mu, res, pk, ztx, zrx, crx, ytx, yrx,
    yn, yp, zn, zp, xn, xp, dd, hres, hyn, hyp, hzn, hzp, hxn, hxp,
    v1, v2, v3, h0, h1, h2, h3, qq, hq, sb, rb,
    load_sem, send_sem, recv_sem, psend, precv,
):
    s = lax.axis_index("sub")
    gy = lax.axis_index("gy")
    gz = lax.axis_index("gz")
    ny = lax.axis_size("gy")
    nz = lax.axis_size("gz")
    subs = lax.axis_size("sub")
    has = {-1: gy > 0, 1: gy < ny - 1}
    hasz = {-1: gz > 0, 1: gz < nz - 1}

    def there(dy, dz):
        ok = None
        for flag in ([has[dy]] if dy else []) + ([hasz[dz]] if dz else []):
            ok = flag if ok is None else jnp.logical_and(ok, flag)
        return ok

    loads = [
        pltpu.make_async_copy(src.at[0], dst.at[:, pl.ds(TOP, N)], load_sem.at[i])
        for i, (src, dst) in enumerate(((classes, cl), (start, xs), (source, rh), (mults, mu)))
    ]
    small = [
        pltpu.make_async_copy(table_hbm, table, load_sem.at[4]),
        pltpu.make_async_copy(chain_hbm, chain, load_sem.at[5]),
    ]
    for copy in small + loads:
        copy.start()

    barrier = pltpu.get_barrier_semaphore()
    greeted = jnp.int32(subs - 1)
    for dy, dz in DIRECTIONS:
        ok = there(dy, dz)
        greeted = greeted + jnp.where(ok, 1, 0)

        @pl.when(ok)
        def _(dy=dy, dz=dz):
            pl.semaphore_signal(barrier, inc=1, device_id=(s, gy + dy, gz + dz), device_id_type=MESH)

    others = [lax.rem(s + d, subs) for d in range(1, 4)]
    for other in others:
        pl.semaphore_signal(barrier, inc=1, device_id=(other, gy, gz), device_id_type=MESH)

    ones = jnp.ones((8, N), jnp.float32)
    zeros = jnp.zeros((8, N), jnp.float32)
    endless = jnp.full((8, N), jnp.inf, jnp.float32)
    blank = jnp.where(lanes(8) // 32 == 1, endless, zeros)
    for side, dy in ((0, -1), (1, 1)):

        @pl.when(jnp.logical_not(has[dy]))
        def _(side=side):
            for i in range(PLANES // 2):
                yrx[side, i] = endless if i in (2, 3) else zeros

        for other, dz in ((0, -1), (1, 1)):

            @pl.when(jnp.logical_not(there(dy, dz)))
            def _(k=2 * side + other):
                crx[k] = blank

    for side, dz in ((0, -1), (1, 1)):

        @pl.when(jnp.logical_not(hasz[dz]))
        def _(side=side):
            for r in range(0, N // 2, 8):
                zrx[side, pl.ds(r, 8)] = blank

    for r in (0, 8, BOTTOM, ROWS - 8):
        for l in range(CX):
            for ref in (xs, rh, v1, v2, v3):
                ref[l, pl.ds(r, 8)] = zeros
            res[l, pl.ds(r, 8)] = ones
    for r in (0, ROWS - 8):
        for ref in (h0, h1, h2, h3):
            ref[pl.ds(r, 8)] = zeros
        hres[pl.ds(r, 8)] = ones

    for copy in small:
        copy.wait()
    my_place = chain[s]
    lower = jnp.float32(0.0)
    upper = jnp.float32(0.0)
    for t in range(4):
        lower = lower + jnp.where(chain[t] == my_place - 1, 1.0, 0.0)
        upper = upper + jnp.where(chain[t] == my_place + 1, 1.0, 0.0)

    splats = [0.5 * inverse(jnp.full((8, N), table[i], jnp.float32)) for i in range(8)]
    splats = [v[:1] for v in splats]

    group = lanes(N) // 8
    loads[0].wait()
    for l in range(CX):
        for r in (TOP, BOTTOM - 8):
            res[l, pl.ds(r, 8)] = lookup(cl[l, pl.ds(r, 8)], splats)
    packed = jnp.zeros((N, N), jnp.int32)
    for l in range(CX):
        packed = jnp.where(group == 4 + l, pltpu.roll(cl[l, pl.ds(TOP, N)], 32 + 8 * l + 4, 1), packed)
    packed = jnp.where(group // 4 == 1, lookup(packed, splats), 0.0)
    loads[1].wait()
    for l in range(CX):
        packed = jnp.where(group == l, pltpu.roll(xs[l, pl.ds(TOP, N)], 8 * l + 4, 1), packed)
    loads[2].wait()
    loads[3].wait()
    rh[0, pl.ds(TOP, N)] = rh[0, pl.ds(TOP, N)] + lower * mu[0, pl.ds(TOP, N)]
    rh[CX - 1, pl.ds(TOP, N)] = rh[CX - 1, pl.ds(TOP, N)] + upper * mu[1, pl.ds(TOP, N)]
    for l in range(CX):
        packed = jnp.where(group == 8 + l, pltpu.roll(rh[l, pl.ds(TOP, N)], 64 + 8 * l + 4, 1), packed)
    pk[...] = packed
    half = N // 2
    place = lanes(half) % 8
    ztx[1] = jnp.where(place < 4, packed[:half], pltpu.roll(packed[half:], 4, 1))
    ztx[0] = jnp.where(place < 4, pltpu.roll(packed[half:], N - 4, 1), packed[:half])
    planes = [(ref, l) for ref in (xs, res, rh) for l in range(CX)]
    row = lax.broadcasted_iota(jnp.int32, (8, N), 0)
    for i in range(PLANES // 2):
        (ref, l), (mate, m) = planes[2 * i], planes[2 * i + 1]
        ytx[0, i] = jnp.where(row < 4, ref[l, pl.ds(TOP, 8)], mate[m, pl.ds(TOP - 4, 8)])
        ytx[1, i] = jnp.where(row < 4, ref[l, pl.ds(BOTTOM - 4, 8)], mate[m, pl.ds(BOTTOM - 8, 8)])

    pl.semaphore_wait(barrier, greeted)

    sent = []
    for k, (dy, dz) in enumerate(DIRECTIONS):
        if dy and dz:
            src = pk.at[pl.ds(0 if dy < 0 else N - 8, 8)]
            dst = crx.at[(2 if dy < 0 else 0) + (1 if dz < 0 else 0)]
        elif dz:
            src, dst = ztx.at[0 if dz < 0 else 1], zrx.at[1 if dz < 0 else 0]
        else:
            src, dst = ytx.at[0 if dy < 0 else 1], yrx.at[1 if dy < 0 else 0]
        copy = pltpu.make_async_remote_copy(
            src_ref=src, dst_ref=dst, send_sem=send_sem.at[k], recv_sem=recv_sem.at[k],
            device_id=(s, gy + dy, gz + dz), device_id_type=MESH,
        )
        pl.when(there(dy, dz))(copy.start)
        sent.append((copy, dy, dz))

    for l in range(CX):
        res[l, pl.ds(TOP + 8, N - 16)] = lookup(cl[l, pl.ds(TOP + 8, N - 16)], splats)

    def inner_links(r, n):
        last_lane = lanes(n) == N - 1
        rc = [res[l, pl.ds(r, n)] for l in range(CX)]
        links = [inverse(rc[l] + rc[l + 1]) for l in range(CX - 1)]
        for l in range(CX):
            c = jnp.where(last_lane, 0.0, inverse(rc[l] + pltpu.roll(rc[l], N - 1, 1)))
            d = pltpu.roll(c, 1, 1)
            total = CAPACITY + c + d
            if l > 0:
                total = total + links[l - 1]
            else:
                total = total + (lower * ROBIN + (1.0 - lower) * inverse(rc[l]))
            if l < CX - 1:
                total = total + links[l]
                xn[l, pl.ds(r, n)] = links[l]
            else:
                total = total + (upper * ROBIN + (1.0 - upper) * inverse(rc[l]))
            zn[l, pl.ds(r, n)] = c
            zp[l, pl.ds(r, n)] = d
            dd[l, pl.ds(r, n)] = total
        hyn[pl.ds(r, n)] = swapped(edge_columns(rc))

    inner_links(TOP, N)

    for copy, dy, dz in sent:
        pl.when(there(-dy, -dz))(copy.wait_recv)

    for side, at in ((0, TOP - 4), (1, BOTTOM)):
        for i, (ref, l) in enumerate(planes):
            ref[l, pl.ds(at, 4)] = yrx[side, i // 2, pl.ds(4 * (i % 2), 4)]
    for r in (FIRST, BOTTOM):
        inner_links(r, 8)

    r, n = FIRST, COUNT
    lane = lanes(n)
    group = lane // 8
    place = lane % 8
    first_lane = lane == 0
    last_lane = lane == N - 1

    low, high = zrx[0], zrx[1]
    near_place = lanes(half) % 8 < 4
    small_place = lanes(8) % 8 < 4
    beside_all = jnp.concatenate(
        [
            jnp.where(small_place, crx[0], crx[1]),
            jnp.where(near_place, low, high),
            jnp.where(near_place, pltpu.roll(low, N - 4, 1), pltpu.roll(high, 4, 1)),
            jnp.where(small_place, crx[2], crx[3]),
        ],
        axis=0,
    )
    hc = jnp.where(lane < 32, pltpu.roll(beside_all, 96, 1), 1.0)
    hres[pl.ds(r, n)] = hc
    h0[pl.ds(r, n)] = jnp.where(lane < 32, beside_all, 0.0)
    hrhs = jnp.where(lane < 32, pltpu.roll(beside_all, 64, 1), 0.0)
    gate = jnp.where((place == 3) | (place == 4), inverse(hc + hyn[pl.ds(r, n)]), 0.0)
    c = jnp.where((place == 3) | (place == 7), 0.0, inverse(hc + pltpu.roll(hc, N - 1, 1)))
    d = pltpu.roll(c, 1, 1)
    c = jnp.where(place == 3, gate, c)
    d = jnp.where(place == 4, gate, d)
    a = inverse(hc + hres[pl.ds(r + 1, n)])
    b = inverse(hc + hres[pl.ds(r - 1, n)])
    f = jnp.where(group < CX - 1, inverse(hc + pltpu.roll(hc, N - 8, 1)), 0.0)
    g = jnp.where(group > 0, pltpu.roll(f, 8, 1), 0.0)
    ends = inverse(hc)
    total = CAPACITY + a + b + c + d + f + g
    total = total + jnp.where(group == 0, lower * ROBIN + (1.0 - lower) * ends, 0.0)
    total = total + jnp.where(group == CX - 1, upper * ROBIN + (1.0 - upper) * ends, 0.0)
    e = inverse(total)
    hyn[pl.ds(r, n)] = a * e
    hyp[pl.ds(r, n)] = b * e
    hzn[pl.ds(r, n)] = c * e
    hzp[pl.ds(r, n)] = d * e
    hxn[pl.ds(r, n)] = f * e
    hxp[pl.ds(r, n)] = g * e
    hq[pl.ds(r, n)] = hrhs * e

    gate = swapped(gate)
    links = [xn[l, pl.ds(r, n)] for l in range(CX - 1)]
    for l in range(CX):
        rc = res[l, pl.ds(r, n)]
        across = pltpu.roll(gate, N - (8 * l + 4), 1)
        a = inverse(rc + res[l, pl.ds(r + 1, n)])
        b = inverse(rc + res[l, pl.ds(r - 1, n)])
        e = inverse(dd[l, pl.ds(r, n)] + a + b + jnp.where(first_lane | last_lane, across, 0.0))
        yn[l, pl.ds(r, n)] = a * e
        yp[l, pl.ds(r, n)] = b * e
        zn[l, pl.ds(r, n)] = jnp.where(last_lane, across, zn[l, pl.ds(r, n)]) * e
        zp[l, pl.ds(r, n)] = jnp.where(first_lane, across, zp[l, pl.ds(r, n)]) * e
        if l > 0:
            xp[l, pl.ds(r, n)] = links[l - 1] * e
        if l < CX - 1:
            xn[l, pl.ds(r, n)] = links[l] * e
        qq[l, pl.ds(r, n)] = rh[l, pl.ds(r, n)] * e

    center = (HIGH_BOUND + LOW_BOUND) / 2.0
    half = (HIGH_BOUND - LOW_BOUND) / 2.0
    sigma = center / half
    rho = 1.0 / sigma
    sends = []
    steps = ((xs, h0), (v1, h1), (v2, h2), (v3, h3))
    for sweep in range(SWEEPS):
        if sweep == 0:
            keep, gain = 0.0, 1.0 / center
        else:
            rho_new = 1.0 / (2.0 * sigma - rho)
            keep, gain = rho_new * rho, 2.0 * rho_new / half
            rho = rho_new
        last = sweep == SWEEPS - 1
        old, hold = steps[sweep]
        if last:
            r, n = TOP, N
            lane = lanes(n)
            first_lane = lane == 0
            last_lane = lane == N - 1
        vs = [old[l, pl.ds(r, n)] for l in range(CX)]
        hv = hold[pl.ds(r, n)]
        ends = []
        for l in range(CX):
            outer = pltpu.roll(hv, N - (8 * l + 4), 1)
            near = yn[l, pl.ds(r, n)] * old[l, pl.ds(r + 1, n)]
            near = near + yp[l, pl.ds(r, n)] * old[l, pl.ds(r - 1, n)]
            near = near + zn[l, pl.ds(r, n)] * pltpu.roll(jnp.where(first_lane, outer, vs[l]), N - 1, 1)
            near = near + zp[l, pl.ds(r, n)] * pltpu.roll(jnp.where(last_lane, outer, vs[l]), 1, 1)
            if l > 0:
                near = near + xp[l, pl.ds(r, n)] * vs[l - 1]
            if l < CX - 1:
                near = near + xn[l, pl.ds(r, n)] * vs[l + 1]
            q = qq[l, pl.ds(r, n)] - vs[l] + near
            if last:
                field = xs[l, pl.ds(r, n)] + v1[l, pl.ds(r, n)] + v2[l, pl.ds(r, n)]
                field = field + (vs[l] + (keep * vs[l] + gain * q))
                t_out[0, l] = field
                if l == 0:
                    ends.append(2.0 * ROBIN * field - mu[0, pl.ds(r, n)])
                if l == CX - 1:
                    ends.append(2.0 * ROBIN * field - mu[1, pl.ds(r, n)])
            else:
                qq[l, pl.ds(r, n)] = q
                steps[sweep + 1][0][l, pl.ds(r, n)] = gain * q if sweep == 0 else keep * vs[l] + gain * q
        if not last:
            edge = edge_columns(vs)
            near = hyn[pl.ds(r, n)] * hold[pl.ds(r + 1, n)] + hyp[pl.ds(r, n)] * hold[pl.ds(r - 1, n)]
            near = near + hzn[pl.ds(r, n)] * pltpu.roll(jnp.where(place == 4, edge, hv), N - 1, 1)
            near = near + hzp[pl.ds(r, n)] * pltpu.roll(jnp.where(place == 3, edge, hv), 1, 1)
            near = near + hxn[pl.ds(r, n)] * pltpu.roll(hv, N - 8, 1) + hxp[pl.ds(r, n)] * pltpu.roll(hv, 8, 1)
            q = hq[pl.ds(r, n)] - hv + near
            hq[pl.ds(r, n)] = q
            steps[sweep + 1][1][pl.ds(r, n)] = gain * q if sweep == 0 else keep * hv + gain * q

    for j in (1, 0, 2):
        above = jnp.where(chain[others[j]] == my_place + 1, 1.0, 0.0)
        sb[j] = above * ends[1] + (1.0 - above) * ends[0]
        copy = pltpu.make_async_remote_copy(
            src_ref=sb.at[j], dst_ref=rb.at[j], send_sem=psend.at[j], recv_sem=precv.at[j],
            device_id=(others[j], gy, gz), device_id_type=MESH,
        )
        copy.start()
        sends.append(copy)

    for copy, dy, dz in sent:
        pl.when(there(dy, dz))(copy.wait_send)
    for copy in sends:
        copy.wait_recv()
    for side, shift in ((0, -1), (1, 1)):
        total = None
        for j in range(3):
            giver = lax.rem(s + subs - (j + 1), subs)
            mine = jnp.where(chain[giver] == my_place + shift, 1.0, 0.0) * rb[j]
            total = mine if total is None else total + mine
        m_out[0, side] = total
    for copy in sends:
        copy.wait_send()


def shards(source, start_field, classes, class_table, chain_place, multipliers):
    wide = pltpu.VMEM((CX, ROWS, N), jnp.float32)
    tall = pltpu.VMEM((ROWS, N), jnp.float32)
    outside = pl.BlockSpec(memory_space=pltpu.HBM)
    inside = pl.BlockSpec(memory_space=pltpu.VMEM)
    arrays = (source, start_field, classes, class_table, chain_place, multipliers)
    arrays = [pltpu.with_memory_space_constraint(x, pltpu.HBM) for x in arrays]
    return pl.pallas_call(
        kernel,
        out_shape=(
            pltpu.VMEM((1, CX, N, N), jnp.float32),
            pltpu.VMEM((1, 2, N, N), jnp.float32),
        ),
        in_specs=[outside] * 6,
        out_specs=(inside, inside),
        scratch_shapes=[
            pltpu.SMEM((8,), jnp.float32), pltpu.SMEM((4,), jnp.int32),
            wide, pltpu.VMEM((CX, ROWS, N), jnp.int32), wide, pltpu.VMEM((2, ROWS, N), jnp.float32), wide,
            pltpu.VMEM((N, N), jnp.float32),
            pltpu.VMEM((2, N // 2, N), jnp.float32), pltpu.VMEM((2, N // 2, N), jnp.float32),
            pltpu.VMEM((4, 8, N), jnp.float32),
            pltpu.VMEM((2, PLANES // 2, 8, N), jnp.float32), pltpu.VMEM((2, PLANES // 2, 8, N), jnp.float32),
            wide, wide, wide, wide, wide, wide, wide, tall, tall, tall, tall, tall, tall, tall,
            wide, wide, wide, tall, tall, tall, tall, wide, tall,
            pltpu.VMEM((3, N, N), jnp.float32), pltpu.VMEM((3, N, N), jnp.float32),
            pltpu.SemaphoreType.DMA((6,)), pltpu.SemaphoreType.DMA((8,)), pltpu.SemaphoreType.DMA((8,)),
            pltpu.SemaphoreType.DMA((3,)), pltpu.SemaphoreType.DMA((3,)),
        ],
        compiler_params=pltpu.CompilerParams(
            collective_id=0, has_side_effects=True, vmem_limit_bytes=32 * 1024 * 1024
        ),
    )(*arrays)


def solution(mesh):
    blocks = P("sub", None, "gy", "gz")
    return jax.shard_map(
        shards,
        mesh=mesh,
        in_specs=(blocks, blocks, blocks, P(), P(), blocks),
        out_specs=(blocks, blocks),
        check_vma=False,
    )
```

time: 123 us -> 24.3 us (0.20)
  the two profiles are of different devices: /device:TPU:262 before, /device:TPU:2 now
where the time goes in v2:
time: 24.3 us; the launch traced here: 24.1 us
  Pallas kernels  22.1 us (91%)
  local copies, waits for them, and re-layouts  1.36 us (6%)
  between operations  0.64 us (3%)
    pallas_call x1, Pallas kernels, shards(): pl.pallas_call(kernel, out_shape=(pltpu.VMEM((1, CX, N, N), jnp.float32),...  22.1 us
    unnamed x2, local copies, waits for them, and re-layouts  1.36 us

profile of v2, /device:TPU:2, one launch (start us, length us, event | category | flops | bytes accessed | tf_op | source)
XLA Modules:
  0.0 24.1 jit_solution(15799102892451624428)
XLA Ops:
  0.6 22.1 %shard_map.77 = (f32[1,4,128,128]{3,2,1,0:T(8,128)S(1)}, f32[1,2,128,128]{3,2,1,0:T(8,128)S(1)}) custom-call(f32[1,4,128,128]{3,2,1,0:T(8,128)} %source.1, f32[1,4,128,128]{3,2,1,0:T(8,128)} %start.1, s32[1,4,128,128]{3,2,1,0:T(8,128)} %classes.1, f32[8]{0:T(128)} %table_hbm.1, s32[4]{0:T(128)} %chain_hbm.1, f32[1,2,128,128]{3,2,1,0:T(8,128)} %mults.1), custom_call_target="tpu_custom_call" | custom-call | tf_op jit(solution)/shard_map/pallas_call | solution.py:383
  22.8 0.7 %copy.10 = f32[1,4,128,128]{3,2,1,0:T(8,128)} copy(f32[1,4,128,128]{3,2,1,0:T(8,128)S(1)} %get-tuple-element.2) | data formatting | bytes 524288
  23.5 0.7 %copy.11 = f32[1,2,128,128]{3,2,1,0:T(8,128)} copy(f32[1,2,128,128]{3,2,1,0:T(8,128)S(1)} %get-tuple-element.3) | data formatting | bytes 262144

commit v3 on v2

--- a/solution.py
+++ b/solution.py
@@ -298,6 +298,17 @@
     sigma = center / half
     rho = 1.0 / sigma
     sends = []
+    def send_packs(ends):
+        for j in (1, 0, 2):
+            above = jnp.where(chain[others[j]] == my_place + 1, 1.0, 0.0)
+            sb[j] = above * ends[1] + (1.0 - above) * ends[0]
+            copy = pltpu.make_async_remote_copy(
+                src_ref=sb.at[j], dst_ref=rb.at[j], send_sem=psend.at[j], recv_sem=precv.at[j],
+                device_id=(others[j], gy, gz), device_id_type=MESH,
+            )
+            copy.start()
+            sends.append(copy)
+
     steps = ((xs, h0), (v1, h1), (v2, h2), (v3, h3))
     for sweep in range(SWEEPS):
         if sweep == 0:
@@ -316,12 +327,11 @@
         vs = [old[l, pl.ds(r, n)] for l in range(CX)]
         hv = hold[pl.ds(r, n)]
         ends = []
-        for l in range(CX):
-            outer = pltpu.roll(hv, N - (8 * l + 4), 1)
+        for l in (0, CX - 1, 1, 2):
             near = yn[l, pl.ds(r, n)] * old[l, pl.ds(r + 1, n)]
             near = near + yp[l, pl.ds(r, n)] * old[l, pl.ds(r - 1, n)]
-            near = near + zn[l, pl.ds(r, n)] * pltpu.roll(jnp.where(first_lane, outer, vs[l]), N - 1, 1)
-            near = near + zp[l, pl.ds(r, n)] * pltpu.roll(jnp.where(last_lane, outer, vs[l]), 1, 1)
+            near = near + zn[l, pl.ds(r, n)] * jnp.where(last_lane, pltpu.roll(hv, N - 1 - (8 * l + 4), 1), pltpu.roll(vs[l], N - 1, 1))
+            near = near + zp[l, pl.ds(r, n)] * jnp.where(first_lane, pltpu.roll(hv, N - (8 * l + 3), 1), pltpu.roll(vs[l], 1, 1))
             if l > 0:
                 near = near + xp[l, pl.ds(r, n)] * vs[l - 1]
             if l < CX - 1:
@@ -335,6 +345,7 @@
                     ends.append(2.0 * ROBIN * field - mu[0, pl.ds(r, n)])
                 if l == CX - 1:
                     ends.append(2.0 * ROBIN * field - mu[1, pl.ds(r, n)])
+                    send_packs(ends)
             else:
                 qq[l, pl.ds(r, n)] = q
                 steps[sweep + 1][0][l, pl.ds(r, n)] = gain * q if sweep == 0 else keep * vs[l] + gain * q
@@ -347,16 +358,6 @@
             q = hq[pl.ds(r, n)] - hv + near
             hq[pl.ds(r, n)] = q
             steps[sweep + 1][1][pl.ds(r, n)] = gain * q if sweep == 0 else keep * hv + gain * q
-
-    for j in (1, 0, 2):
-        above = jnp.where(chain[others[j]] == my_place + 1, 1.0, 0.0)
-        sb[j] = above * ends[1] + (1.0 - above) * ends[0]
-        copy = pltpu.make_async_remote_copy(
-            src_ref=sb.at[j], dst_ref=rb.at[j], send_sem=psend.at[j], recv_sem=precv.at[j],
-            device_id=(others[j], gy, gz), device_id_type=MESH,
-        )
-        copy.start()
-        sends.append(copy)
 
     for copy, dy, dz in sent:
         pl.when(there(dy, dz))(copy.wait_send)

time: 24.3 us -> 23.7 us (0.975)
  Pallas kernels: 22.1 us -> 21.6 us
    pallas_call x1, Pallas kernels: 22.1 us -> 21.6 us  [shards(): pl.pallas_call(kernel, out_shape=(pltpu.VMEM((1, CX, N, N), jnp.float32),...]
where the time goes in v3:
time: 23.7 us; the launch traced here: 23.6 us
  Pallas kernels  21.6 us (91%)
  local copies, waits for them, and re-layouts  1.36 us (6%)
  between operations  0.64 us (3%)
    pallas_call x1, Pallas kernels, shards(): pl.pallas_call(kernel, out_shape=(pltpu.VMEM((1, CX, N, N), jnp.float32),...  21.6 us
    unnamed x2, local copies, waits for them, and re-layouts  1.36 us

profile of v3, /device:TPU:2, one launch (start us, length us, event | category | flops | bytes accessed | tf_op | source)
XLA Modules:
  0.0 23.6 jit_solution(16575738773868457275)
XLA Ops:
  0.6 21.6 %shard_map.77 = (f32[1,4,128,128]{3,2,1,0:T(8,128)S(1)}, f32[1,2,128,128]{3,2,1,0:T(8,128)S(1)}) custom-call(f32[1,4,128,128]{3,2,1,0:T(8,128)} %source.1, f32[1,4,128,128]{3,2,1,0:T(8,128)} %start.1, s32[1,4,128,128]{3,2,1,0:T(8,128)} %classes.1, f32[8]{0:T(128)} %table_hbm.1, s32[4]{0:T(128)} %chain_hbm.1, f32[1,2,128,128]{3,2,1,0:T(8,128)} %mults.1), custom_call_target="tpu_custom_call" | custom-call | tf_op jit(solution)/shard_map/pallas_call | solution.py:384
  22.2 0.7 %copy.10 = f32[1,4,128,128]{3,2,1,0:T(8,128)} copy(f32[1,4,128,128]{3,2,1,0:T(8,128)S(1)} %get-tuple-element.2) | data formatting | bytes 524288
  22.9 0.7 %copy.11 = f32[1,2,128,128]{3,2,1,0:T(8,128)} copy(f32[1,2,128,128]{3,2,1,0:T(8,128)S(1)} %get-tuple-element.3) | data formatting | bytes 262144

commit v4 on v3

v4 whole, which is shorter than its diff:
```python
import jax
import jax.numpy as jnp
from jax import lax
from jax.experimental import pallas as pl
from jax.experimental.pallas import tpu as pltpu
from jax.sharding import PartitionSpec as P

SWEEPS = 4
ROBIN = 1.0
CAPACITY = 0.5
LOW_BOUND = 0.1
HIGH_BOUND = 2.0
MESH = pl.DeviceIdType.MESH

CX = 4
N = 128
TOP = 16
BOTTOM = TOP + N
ROWS = BOTTOM + 16
FIRST, COUNT = 8, N + 16
QUARTER = N // 4
HIGH = QUARTER + 16
PLANES = 12
DIRECTIONS = ((-1, -1), (-1, 1), (1, -1), (1, 1), (0, 1), (0, -1), (-1, 0), (1, 0))


def inverse(x):
    return pltpu.reciprocal(x, approx=True)


def lookup(classes, splats):
    bit0 = (classes & 1) == 1
    bit1 = (classes & 2) == 2
    bit2 = classes >= 4
    pairs = [jnp.where(bit0, splats[i + 1], splats[i]) for i in range(0, 8, 2)]
    quads = [jnp.where(bit1, pairs[i + 1], pairs[i]) for i in (0, 2)]
    return jnp.where(bit2, quads[1], quads[0])


def lanes(n):
    return lax.broadcasted_iota(jnp.int32, (n, N), 1)


def edge_columns(ref):
    group = lanes(QUARTER) // 8
    body = None
    for k in range(4):
        for l in range(CX):
            turned = pltpu.roll(ref[l, pl.ds(TOP + QUARTER * k, QUARTER)], QUARTER * k + 8 * l + 4, 1)
            body = turned if body is None else jnp.where(group == 4 * k + l, turned, body)
    group = lanes(8) // 8
    above = pltpu.roll(body[QUARTER - 8 :], QUARTER, 1)
    below = pltpu.roll(body[:8], N - QUARTER, 1)
    for l in range(CX):
        above = jnp.where(group == l, pltpu.roll(ref[l, pl.ds(TOP - 8, 8)], 8 * l + 4, 1), above)
        below = jnp.where(group == 12 + l, pltpu.roll(ref[l, pl.ds(BOTTOM, 8)], 96 + 8 * l + 4, 1), below)
    return jnp.concatenate([above, body, below], axis=0)


def turned_in(h, l, whole):
    parts = [pltpu.roll(h[8 : 8 + QUARTER], N - (QUARTER * k + 8 * l + 4), 1) for k in range(4)]
    if whole:
        above = pltpu.roll(h[:8], N - (8 * l + 4), 1)
        below = pltpu.roll(h[8 + QUARTER :], N - (96 + 8 * l + 4), 1)
        parts = [above] + parts + [below]
    return jnp.concatenate(parts, axis=0)


def kernel(
    source, start, classes, table_hbm, chain_hbm, mults, t_out, m_out,
    table, chain, xs, cl, rh, mu, res, ctx, crx, ztx, zrx, ytx, yrx,
    yl, zn, zp, xl, dd, ee, rr, v1, v2, v3, hres, h0, h1, h2, h3, sb, rb,
    load_sem, send_sem, recv_sem, psend, precv,
):
    s = lax.axis_index("sub")
    gy = lax.axis_index("gy")
    gz = lax.axis_index("gz")
    ny = lax.axis_size("gy")
    nz = lax.axis_size("gz")
    subs = lax.axis_size("sub")
    has = {-1: gy > 0, 1: gy < ny - 1}
    hasz = {-1: gz > 0, 1: gz < nz - 1}

    def there(dy, dz):
        ok = None
        for flag in ([has[dy]] if dy else []) + ([hasz[dz]] if dz else []):
            ok = flag if ok is None else jnp.logical_and(ok, flag)
        return ok

    loads = [
        pltpu.make_async_copy(src.at[0], dst.at[:, pl.ds(TOP, N)], load_sem.at[i])
        for i, (src, dst) in enumerate(((classes, cl), (start, xs), (source, rh), (mults, mu)))
    ]
    small = [
        pltpu.make_async_copy(table_hbm, table, load_sem.at[4]),
        pltpu.make_async_copy(chain_hbm, chain, load_sem.at[5]),
    ]
    for copy in small + loads:
        copy.start()

    barrier = pltpu.get_barrier_semaphore()
    greeted = jnp.int32(subs - 1)
    for dy, dz in DIRECTIONS:
        ok = there(dy, dz)
        greeted = greeted + jnp.where(ok, 1, 0)

        @pl.when(ok)
        def _(dy=dy, dz=dz):
            pl.semaphore_signal(barrier, inc=1, device_id=(s, gy + dy, gz + dz), device_id_type=MESH)

    others = [lax.rem(s + d, subs) for d in range(1, 4)]
    for other in others:
        pl.semaphore_signal(barrier, inc=1, device_id=(other, gy, gz), device_id_type=MESH)

    ones = jnp.ones((8, N), jnp.float32)
    zeros = jnp.zeros((8, N), jnp.float32)
    endless = jnp.full((8, N), jnp.inf, jnp.float32)
    blank = jnp.where(lanes(8) // 32 == 1, endless, zeros)
    for side, dy in ((0, -1), (1, 1)):

        @pl.when(jnp.logical_not(has[dy]))
        def _(side=side):
            for i in range(PLANES // 2):
                yrx[side, i] = endless if i in (2, 3) else zeros

        for other, dz in ((0, -1), (1, 1)):

            @pl.when(jnp.logical_not(there(dy, dz)))
            def _(k=2 * side + other):
                crx[k] = blank

    for side, dz in ((0, -1), (1, 1)):

        @pl.when(jnp.logical_not(hasz[dz]))
        def _(side=side):
            for a in range(3):
                for r in range(0, QUARTER // 2, 8):
                    zrx[side, a, pl.ds(r, 8)] = endless if a == 1 else zeros

    for r in (0, 8, BOTTOM, ROWS - 8):
        for l in range(CX):
            for ref in (xs, rh, yl, v1, v2, v3):
                ref[l, pl.ds(r, 8)] = zeros
            res[l, pl.ds(r, 8)] = endless if r in (8, BOTTOM) else ones
    for r in (0, 8 + HIGH):
        for ref in (h0, h1, h2, h3):
            ref[pl.ds(r, 8)] = zeros
        hres[pl.ds(r, 8)] = ones

    for copy in small:
        copy.wait()
    my_place = chain[s]
    lower = jnp.float32(0.0)
    upper = jnp.float32(0.0)
    for t in range(4):
        lower = lower + jnp.where(chain[t] == my_place - 1, 1.0, 0.0)
        upper = upper + jnp.where(chain[t] == my_place + 1, 1.0, 0.0)

    splats = [0.5 * inverse(jnp.full((8, N), table[i], jnp.float32)) for i in range(8)]
    splats = [v[:1] for v in splats]

    lane = lanes(QUARTER)
    group = lane // 8
    place = lane % 8

    def outer_columns(ref):
        packed = None
        for k in range(4):
            for l in range(CX):
                turned = pltpu.roll(ref[l, pl.ds(TOP + QUARTER * k, QUARTER)], QUARTER * k + 8 * l + 4, 1)
                packed = turned if packed is None else jnp.where(group == 4 * k + l, turned, packed)
        return jnp.take_along_axis(packed, lane ^ 7, axis=1)

    loads[0].wait()
    for l in range(CX):
        for r in (TOP, BOTTOM - 8):
            res[l, pl.ds(r, 8)] = lookup(cl[l, pl.ds(r, 8)], splats)
    packed_res = lookup(outer_columns(cl), splats)
    loads[1].wait()
    packed_xs = outer_columns(xs)
    loads[2].wait()
    loads[3].wait()
    rh[0, pl.ds(TOP, N)] = rh[0, pl.ds(TOP, N)] + lower * mu[0, pl.ds(TOP, N)]
    rh[CX - 1, pl.ds(TOP, N)] = rh[CX - 1, pl.ds(TOP, N)] + upper * mu[1, pl.ds(TOP, N)]
    packed_rh = outer_columns(rh)
    half = QUARTER // 2
    near_side = place[:half] < 4
    group8 = lanes(8) // 32
    up_corner = down_corner = None
    for a, packed in enumerate((packed_xs, packed_res, packed_rh)):
        ztx[0, a] = jnp.where(near_side, packed[:half], pltpu.roll(packed[half:], 4, 1))
        ztx[1, a] = jnp.where(near_side, pltpu.roll(packed[half:], N - 4, 1), packed[:half])
        first = packed[:8] if a == 0 else pltpu.roll(packed[:8], 32 * a, 1)
        final = pltpu.roll(packed[QUARTER - 8 :], 32 * a + 32, 1)
        up_corner = first if a == 0 else jnp.where(group8 == a, first, up_corner)
        down_corner = final if a == 0 else jnp.where(group8 == a, final, down_corner)
    ctx[0] = up_corner
    ctx[1] = down_corner
    planes = [(ref, l) for ref in (xs, res, rh) for l in range(CX)]
    row = lax.broadcasted_iota(jnp.int32, (8, N), 0)
    for i in range(PLANES // 2):
        (ref, l), (mate, m) = planes[2 * i], planes[2 * i + 1]
        ytx[0, i] = jnp.where(row < 4, ref[l, pl.ds(TOP, 8)], mate[m, pl.ds(TOP - 4, 8)])
        ytx[1, i] = jnp.where(row < 4, ref[l, pl.ds(BOTTOM - 4, 8)], mate[m, pl.ds(BOTTOM - 8, 8)])

    pl.semaphore_wait(barrier, greeted)

    sent = []
    for k, (dy, dz) in enumerate(DIRECTIONS):
        if dy and dz:
            src = ctx.at[0 if dy < 0 else 1]
            dst = crx.at[(2 if dy < 0 else 0) + (1 if dz < 0 else 0)]
        elif dz:
            src, dst = ztx.at[0 if dz < 0 else 1], zrx.at[1 if dz < 0 else 0]
        else:
            src, dst = ytx.at[0 if dy < 0 else 1], yrx.at[1 if dy < 0 else 0]
        copy = pltpu.make_async_remote_copy(
            src_ref=src, dst_ref=dst, send_sem=send_sem.at[k], recv_sem=recv_sem.at[k],
            device_id=(s, gy + dy, gz + dz), device_id_type=MESH,
        )
        pl.when(there(dy, dz))(copy.start)
        sent.append((copy, dy, dz))

    for l in range(CX):
        res[l, pl.ds(TOP + 8, N - 16)] = lookup(cl[l, pl.ds(TOP + 8, N - 16)], splats)

    def cat(ref, l, blocks, shift=0):
        parts = [ref[l, pl.ds(r + shift, n)] for r, n in blocks]
        return parts[0] if len(parts) == 1 else jnp.concatenate(parts, axis=0)

    def put(ref, l, blocks, value):
        at = 0
        for r, n in blocks:
            ref[l, pl.ds(r, n)] = value[at : at + n]
            at += n

    def inner_part(blocks):
        last_lane = lanes(sum(n for _, n in blocks)) == N - 1
        rc = [cat(res, l, blocks) for l in range(CX)]
        vs = [cat(xs, l, blocks) for l in range(CX)]
        links = [inverse(rc[l] + rc[l + 1]) for l in range(CX - 1)]
        for l in range(CX):
            a = inverse(rc[l] + cat(res, l, blocks, 1))
            b = inverse(rc[l] + cat(res, l, blocks, -1))
            c = jnp.where(last_lane, 0.0, inverse(rc[l] + pltpu.roll(rc[l], N - 1, 1)))
            d = pltpu.roll(c, 1, 1)
            total = CAPACITY + a + b + c + d
            near = a * cat(xs, l, blocks, 1) + b * cat(xs, l, blocks, -1)
            near = near + c * pltpu.roll(vs[l], N - 1, 1) + d * pltpu.roll(vs[l], 1, 1)
            if l > 0:
                total = total + links[l - 1]
                near = near + links[l - 1] * vs[l - 1]
            else:
                total = total + (lower * ROBIN + (1.0 - lower) * inverse(rc[l]))
            if l < CX - 1:
                total = total + links[l]
                near = near + links[l] * vs[l + 1]
                put(xl, l, blocks, links[l])
            else:
                total = total + (upper * ROBIN + (1.0 - upper) * inverse(rc[l]))
            put(yl, l, blocks, a)
            put(zn, l, blocks, c)
            put(zp, l, blocks, d)
            put(dd, l, blocks, total)
            put(rr, l, blocks, cat(rh, l, blocks) - total * vs[l] + near)

    inner_part(((TOP, N),))

    for copy, dy, dz in sent:
        pl.when(there(-dy, -dz))(copy.wait_recv)

    for side, at in ((0, TOP - 4), (1, BOTTOM)):
        for i, (ref, l) in enumerate(planes):
            ref[l, pl.ds(at, 4)] = yrx[side, i // 2, pl.ds(4 * (i % 2), 4)]

    center = (HIGH_BOUND + LOW_BOUND) / 2.0
    half_width = (HIGH_BOUND - LOW_BOUND) / 2.0
    sigma = center / half_width
    rho = 1.0 / sigma

    lane = lanes(HIGH)
    place = lane % 8
    layer = lane // 8 % 4
    near_side = lanes(half) % 8 < 4
    lane8 = lanes(8)
    near8 = lane8 % 8 < 4
    up_corner = jnp.where(near8, crx[1], crx[0])
    down_corner = jnp.where(near8, crx[3], crx[2])
    tiles = []
    for a in range(3):
        low, high = zrx[0, a], zrx[1, a]
        upper_rows = jnp.where(near_side, high, low)
        lower_rows = jnp.where(near_side, pltpu.roll(high, N - 4, 1), pltpu.roll(low, 4, 1))
        above = up_corner if a == 0 else pltpu.roll(up_corner, N - 32 * a, 1)
        above = jnp.where(lane8 < 32, above, pltpu.roll(lower_rows[half - 8 :], 32, 1))
        below = jnp.where(lane8 >= 96, pltpu.roll(down_corner, 96 - 32 * a, 1), pltpu.roll(upper_rows[:8], 96, 1))
        tiles.append(jnp.concatenate([above, upper_rows, lower_rows, below], axis=0))
    hv, hc, hrhs = tiles
    hrows = pl.ds(8, HIGH)
    hres[hrows] = hc
    h0[hrows] = hv
    gate = jnp.where((place == 3) | (place == 4), inverse(hc + edge_columns(res)), 0.0)
    hzn = jnp.where((place == 3) | (place == 7), 0.0, inverse(hc + pltpu.roll(hc, N - 1, 1)))
    hzp = pltpu.roll(hzn, 1, 1)
    hxn = jnp.where(layer < CX - 1, inverse(hc + pltpu.roll(hc, N - 8, 1)), 0.0)
    hxp = pltpu.roll(hxn, 8, 1)
    hyn = inverse(hc + hres[pl.ds(9, HIGH)])
    hyp = inverse(hc + hres[pl.ds(7, HIGH)])
    ends = inverse(hc)
    hd = CAPACITY + hyn + hyp + hzn + hzp + hxn + hxp + gate
    hd = hd + jnp.where(layer == 0, lower * ROBIN + (1.0 - lower) * ends, 0.0)
    hd = hd + jnp.where(layer == CX - 1, upper * ROBIN + (1.0 - upper) * ends, 0.0)
    he = inverse(hd)

    def outer_near(hold, hv, old):
        near = hyn * hold[pl.ds(9, HIGH)] + hyp * hold[pl.ds(7, HIGH)]
        near = near + hzn * pltpu.roll(hv, N - 1, 1) + hzp * pltpu.roll(hv, 1, 1)
        near = near + hxn * pltpu.roll(hv, N - 8, 1) + hxp * pltpu.roll(hv, 8, 1)
        return near + gate * edge_columns(old)

    hr = hrhs - hd * hv + outer_near(h0, hv, xs)
    h1[hrows] = 1.0 / center * (he * hr)

    inner_part(((FIRST, 16), (BOTTOM - 8, 16)))
    r, n = FIRST, COUNT
    lane = lanes(n)
    edge = (lane == 0) | (lane == N - 1)
    flow = gate * hv
    for l in range(CX):
        across = jnp.where(edge, turned_in(gate, l, True), 0.0)
        total = dd[l, pl.ds(r, n)] + across
        e = inverse(total)
        q = rr[l, pl.ds(r, n)] - across * xs[l, pl.ds(r, n)] + jnp.where(edge, turned_in(flow, l, True), 0.0)
        dd[l, pl.ds(r, n)] = total
        ee[l, pl.ds(r, n)] = e
        rr[l, pl.ds(r, n)] = q
        v1[l, pl.ds(r, n)] = 1.0 / center * (e * q)

    sends = []

    def send_packs(ends):
        for j in (1, 0, 2):
            above = jnp.where(chain[others[j]] == my_place + 1, 1.0, 0.0)
            sb[j] = above * ends[1] + (1.0 - above) * ends[0]
            copy = pltpu.make_async_remote_copy(
                src_ref=sb.at[j], dst_ref=rb.at[j], send_sem=psend.at[j], recv_sem=precv.at[j],
                device_id=(others[j], gy, gz), device_id_type=MESH,
            )
            copy.start()
            sends.append(copy)

    steps = ((xs, h0), (v1, h1), (v2, h2), (v3, h3))
    for sweep in range(1, SWEEPS):
        rho_new = 1.0 / (2.0 * sigma - rho)
        keep, gain = rho_new * rho, 2.0 * rho_new / half_width
        rho = rho_new
        last = sweep == SWEEPS - 1
        old, hold = steps[sweep]
        if last:
            r, n = TOP, N
            lane = lanes(n)
            edge = (lane == 0) | (lane == N - 1)
        vs = [old[l, pl.ds(r, n)] for l in range(CX)]
        hv = hold[hrows]
        flow = gate * hv
        ends = []
        for l in (0, CX - 1, 1, 2):
            near = yl[l, pl.ds(r, n)] * old[l, pl.ds(r + 1, n)] + yl[l, pl.ds(r - 1, n)] * old[l, pl.ds(r - 1, n)]
            near = near + zn[l, pl.ds(r, n)] * pltpu.roll(vs[l], N - 1, 1)
            near = near + zp[l, pl.ds(r, n)] * pltpu.roll(vs[l], 1, 1)
            if l > 0:
                near = near + xl[l - 1, pl.ds(r, n)] * vs[l - 1]
            if l < CX - 1:
                near = near + xl[l, pl.ds(r, n)] * vs[l + 1]
            near = near + jnp.where(edge, turned_in(flow, l, not last), 0.0)
            q = rr[l, pl.ds(r, n)] - dd[l, pl.ds(r, n)] * vs[l] + near
            step = keep * vs[l] + gain * (ee[l, pl.ds(r, n)] * q)
            if last:
                field = xs[l, pl.ds(r, n)] + v1[l, pl.ds(r, n)] + v2[l, pl.ds(r, n)]
                field = field + (vs[l] + step)
                t_out[0, l] = field
                if l == 0:
                    ends.append(2.0 * ROBIN * field - mu[0, pl.ds(r, n)])
                if l == CX - 1:
                    ends.append(2.0 * ROBIN * field - mu[1, pl.ds(r, n)])
                    send_packs(ends)
            else:
                rr[l, pl.ds(r, n)] = q
                steps[sweep + 1][0][l, pl.ds(r, n)] = step
        if not last:
            hr = hr - hd * hv + outer_near(hold, hv, old)
            steps[sweep + 1][1][hrows] = keep * hv + gain * (he * hr)

    for copy, dy, dz in sent:
        pl.when(there(dy, dz))(copy.wait_send)
    for copy in sends:
        copy.wait_recv()
    for side, shift in ((0, -1), (1, 1)):
        total = None
        for j in range(3):
            giver = lax.rem(s + subs - (j + 1), subs)
            mine = jnp.where(chain[giver] == my_place + shift, 1.0, 0.0) * rb[j]
            total = mine if total is None else total + mine
        m_out[0, side] = total
    for copy in sends:
        copy.wait_send()


def shards(source, start_field, classes, class_table, chain_place, multipliers):
    wide = pltpu.VMEM((CX, ROWS, N), jnp.float32)
    tall = pltpu.VMEM((HIGH + 16, N), jnp.float32)
    outside = pl.BlockSpec(memory_space=pltpu.HBM)
    inside = pl.BlockSpec(memory_space=pltpu.VMEM)
    arrays = (source, start_field, classes, class_table, chain_place, multipliers)
    arrays = [pltpu.with_memory_space_constraint(x, pltpu.HBM) for x in arrays]
    return pl.pallas_call(
        kernel,
        out_shape=(
            pltpu.VMEM((1, CX, N, N), jnp.float32),
            pltpu.VMEM((1, 2, N, N), jnp.float32),
        ),
        in_specs=[outside] * 6,
        out_specs=(inside, inside),
        scratch_shapes=[
            pltpu.SMEM((8,), jnp.float32), pltpu.SMEM((4,), jnp.int32),
            wide, pltpu.VMEM((CX, ROWS, N), jnp.int32), wide, pltpu.VMEM((2, ROWS, N), jnp.float32), wide,
            pltpu.VMEM((2, 8, N), jnp.float32), pltpu.VMEM((4, 8, N), jnp.float32),
            pltpu.VMEM((2, 3, QUARTER // 2, N), jnp.float32), pltpu.VMEM((2, 3, QUARTER // 2, N), jnp.float32),
            pltpu.VMEM((2, PLANES // 2, 8, N), jnp.float32), pltpu.VMEM((2, PLANES // 2, 8, N), jnp.float32),
            wide, wide, wide, wide, wide, wide, wide, wide, wide, wide, tall, tall, tall, tall, tall,
            pltpu.VMEM((3, N, N), jnp.float32), pltpu.VMEM((3, N, N), jnp.float32),
            pltpu.SemaphoreType.DMA((6,)), pltpu.SemaphoreType.DMA((8,)), pltpu.SemaphoreType.DMA((8,)),
            pltpu.SemaphoreType.DMA((3,)), pltpu.SemaphoreType.DMA((3,)),
        ],
        compiler_params=pltpu.CompilerParams(
            collective_id=0, has_side_effects=True, vmem_limit_bytes=32 * 1024 * 1024
        ),
    )(*arrays)


def solution(mesh):
    blocks = P("sub", None, "gy", "gz")
    return jax.shard_map(
        shards,
        mesh=mesh,
        in_specs=(blocks, blocks, blocks, P(), P(), blocks),
        out_specs=(blocks, blocks),
        check_vma=False,
    )
```

time: 23.7 us -> 23.5 us (level)
  no operation moved by 1% of the time
where the time goes in v4:
time: 23.5 us; the launch traced here: 23.4 us
  Pallas kernels  21.4 us (91%)
  local copies, waits for them, and re-layouts  1.36 us (6%)
  between operations  0.64 us (3%)
    pallas_call x1, Pallas kernels, shards(): pl.pallas_call(kernel, out_shape=(pltpu.VMEM((1, CX, N, N), jnp.float32),...  21.4 us
    unnamed x2, local copies, waits for them, and re-layouts  1.36 us

profile of v4, /device:TPU:2, one launch (start us, length us, event | category | flops | bytes accessed | tf_op | source)
XLA Modules:
  0.0 23.4 jit_solution(11848693921031070782)
XLA Ops:
  0.6 21.4 %shard_map.77 = (f32[1,4,128,128]{3,2,1,0:T(8,128)S(1)}, f32[1,2,128,128]{3,2,1,0:T(8,128)S(1)}) custom-call(f32[1,4,128,128]{3,2,1,0:T(8,128)} %source.1, f32[1,4,128,128]{3,2,1,0:T(8,128)} %start.1, s32[1,4,128,128]{3,2,1,0:T(8,128)} %classes.1, f32[8]{0:T(128)} %table_hbm.1, s32[4]{0:T(128)} %chain_hbm.1, f32[1,2,128,128]{3,2,1,0:T(8,128)} %mults.1), custom_call_target="tpu_custom_call" | custom-call | tf_op jit(solution)/shard_map/pallas_call | solution.py:416
  22.0 0.7 %copy.10 = f32[1,4,128,128]{3,2,1,0:T(8,128)} copy(f32[1,4,128,128]{3,2,1,0:T(8,128)S(1)} %get-tuple-element.2) | data formatting | bytes 524288
  22.7 0.7 %copy.11 = f32[1,2,128,128]{3,2,1,0:T(8,128)} copy(f32[1,2,128,128]{3,2,1,0:T(8,128)S(1)} %get-tuple-element.3) | data formatting | bytes 262144

commit v5 on v4

--- a/solution.py
+++ b/solution.py
@@ -1,3 +1,5 @@
+import functools
+
 import jax
 import jax.numpy as jnp
 from jax import lax
@@ -67,7 +69,7 @@
 
 
 def kernel(
-    source, start, classes, table_hbm, chain_hbm, mults, t_out, m_out,
+    unused, source, start, classes, table_hbm, chain_hbm, mults, t_out, m_out,
     table, chain, xs, cl, rh, mu, res, ctx, crx, ztx, zrx, ytx, yrx,
     yl, zn, zp, xl, dd, ee, rr, v1, v2, v3, hres, h0, h1, h2, h3, sb, rb,
     load_sem, send_sem, recv_sem, psend, precv,
@@ -77,7 +79,6 @@
     gz = lax.axis_index("gz")
     ny = lax.axis_size("gy")
     nz = lax.axis_size("gz")
-    subs = lax.axis_size("sub")
     has = {-1: gy > 0, 1: gy < ny - 1}
     hasz = {-1: gz > 0, 1: gz < nz - 1}
 
@@ -98,8 +99,10 @@
     for copy in small + loads:
         copy.start()
 
+    mates = {1: s + 1 - 2 * lax.rem(s, 2), 2: lax.rem(s + 2, 4), 3: 3 - s}
+    mates = {pairing: mates[pairing] for pairing in (2, 1, 3) if pairing != unused}
     barrier = pltpu.get_barrier_semaphore()
-    greeted = jnp.int32(subs - 1)
+    greeted = jnp.int32(len(mates))
     for dy, dz in DIRECTIONS:
         ok = there(dy, dz)
         greeted = greeted + jnp.where(ok, 1, 0)
@@ -108,8 +111,7 @@
         def _(dy=dy, dz=dz):
             pl.semaphore_signal(barrier, inc=1, device_id=(s, gy + dy, gz + dz), device_id_type=MESH)
 
-    others = [lax.rem(s + d, subs) for d in range(1, 4)]
-    for other in others:
+    for other in mates.values():
         pl.semaphore_signal(barrier, inc=1, device_id=(other, gy, gz), device_id_type=MESH)
 
     ones = jnp.ones((8, N), jnp.float32)
@@ -339,12 +341,12 @@
     sends = []
 
     def send_packs(ends):
-        for j in (1, 0, 2):
-            above = jnp.where(chain[others[j]] == my_place + 1, 1.0, 0.0)
+        for j, other in enumerate(mates.values()):
+            above = jnp.where(chain[other] == my_place + 1, 1.0, 0.0)
             sb[j] = above * ends[1] + (1.0 - above) * ends[0]
             copy = pltpu.make_async_remote_copy(
                 src_ref=sb.at[j], dst_ref=rb.at[j], send_sem=psend.at[j], recv_sem=precv.at[j],
-                device_id=(others[j], gy, gz), device_id_type=MESH,
+                device_id=(other, gy, gz), device_id_type=MESH,
             )
             copy.start()
             sends.append(copy)
@@ -397,24 +399,22 @@
         copy.wait_recv()
     for side, shift in ((0, -1), (1, 1)):
         total = None
-        for j in range(3):
-            giver = lax.rem(s + subs - (j + 1), subs)
-            mine = jnp.where(chain[giver] == my_place + shift, 1.0, 0.0) * rb[j]
+        for j, other in enumerate(mates.values()):
+            mine = jnp.where(chain[other] == my_place + shift, 1.0, 0.0) * rb[j]
             total = mine if total is None else total + mine
         m_out[0, side] = total
     for copy in sends:
         copy.wait_send()
 
 
-def shards(source, start_field, classes, class_table, chain_place, multipliers):
+def call(unused, arrays):
     wide = pltpu.VMEM((CX, ROWS, N), jnp.float32)
     tall = pltpu.VMEM((HIGH + 16, N), jnp.float32)
     outside = pl.BlockSpec(memory_space=pltpu.HBM)
     inside = pl.BlockSpec(memory_space=pltpu.VMEM)
-    arrays = (source, start_field, classes, class_table, chain_place, multipliers)
     arrays = [pltpu.with_memory_space_constraint(x, pltpu.HBM) for x in arrays]
     return pl.pallas_call(
-        kernel,
+        functools.partial(kernel, unused),
         out_shape=(
             pltpu.VMEM((1, CX, N, N), jnp.float32),
             pltpu.VMEM((1, 2, N, N), jnp.float32),
@@ -428,14 +428,40 @@
             pltpu.VMEM((2, 3, QUARTER // 2, N), jnp.float32), pltpu.VMEM((2, 3, QUARTER // 2, N), jnp.float32),
             pltpu.VMEM((2, PLANES // 2, 8, N), jnp.float32), pltpu.VMEM((2, PLANES // 2, 8, N), jnp.float32),
             wide, wide, wide, wide, wide, wide, wide, wide, wide, wide, tall, tall, tall, tall, tall,
-            pltpu.VMEM((3, N, N), jnp.float32), pltpu.VMEM((3, N, N), jnp.float32),
+            pltpu.VMEM((2, N, N), jnp.float32), pltpu.VMEM((2, N, N), jnp.float32),
             pltpu.SemaphoreType.DMA((6,)), pltpu.SemaphoreType.DMA((8,)), pltpu.SemaphoreType.DMA((8,)),
-            pltpu.SemaphoreType.DMA((3,)), pltpu.SemaphoreType.DMA((3,)),
+            pltpu.SemaphoreType.DMA((2,)), pltpu.SemaphoreType.DMA((2,)),
         ],
         compiler_params=pltpu.CompilerParams(
-            collective_id=0, has_side_effects=True, vmem_limit_bytes=32 * 1024 * 1024
+            collective_id=unused - 1, has_side_effects=True, vmem_limit_bytes=32 * 1024 * 1024
         ),
     )(*arrays)
+
+
+def pick(chain_hbm, out, chain, sem):
+    copy = pltpu.make_async_copy(chain_hbm, chain, sem)
+    copy.start()
+    copy.wait()
+    out[0] = jnp.int32(0)
+    for t in range(2, 4):
+
+        @pl.when(jnp.abs(chain[t] - chain[0]) == 2)
+        def _(t=t):
+            out[0] = jnp.int32(t - 1)
+
+
+def shards(source, start_field, classes, class_table, chain_place, multipliers):
+    arrays = (source, start_field, classes, class_table, chain_place, multipliers)
+    chain_place = pltpu.with_memory_space_constraint(chain_place, pltpu.HBM)
+    unused = pl.pallas_call(
+        pick,
+        out_shape=pltpu.SMEM((1,), jnp.int32),
+        in_specs=[pl.BlockSpec(memory_space=pltpu.HBM)],
+        out_specs=pl.BlockSpec(memory_space=pltpu.SMEM),
+        scratch_shapes=[pltpu.SMEM((4,), jnp.int32), pltpu.SemaphoreType.DMA],
+    )(chain_place)
+    branches = [functools.partial(call, pairing) for pairing in (1, 2, 3)]
+    return lax.switch(unused[0], branches, arrays)
 
 
 def solution(mesh):

time: 23.5 us -> 23.5 us (level)
  the two profiles are of different devices: /device:TPU:2 before, /device:TPU:19 now
where the time goes in v5:
time: 23.5 us; the launch traced here: 23.4 us
  Pallas kernels  21.4 us (91%)
  local copies, waits for them, and re-layouts  1.36 us (6%)
  between operations  0.65 us (3%)
    pallas_call x1, Pallas kernels, call(): pl.pallas_call(functools.partial(kernel, unused), out_shape=(pltpu.VMEM((...  20.7 us
    unnamed x2, local copies, waits for them, and re-layouts  1.36 us
    pallas_call x1, Pallas kernels, shards(): pl.pallas_call(pick, out_shape=pltpu.SMEM((1,), jnp.int32), in_specs=[pl....  0.68 us

profile of v5, /device:TPU:19, one launch (start us, length us, event | category | flops | bytes accessed | tf_op | source)
XLA Modules:
  0.0 23.4 jit_solution(13753204366773456913)
XLA Ops:
  0.6 0.7 %shard_map.83 = s32[1]{0:T(128)S(4)} custom-call(s32[4]{0:T(128)} %chain_hbm.1), custom_call_target="tpu_custom_call" | custom-call | tf_op jit(solution)/shard_map/pallas_call | solution.py:456
  1.3 20.7 %conditional.1 = ((f32[1,4,128,128]{3,2,1,0:T(8,128)S(1)}, f32[1,2,128,128]{3,2,1,0:T(8,128)S(1)})) conditional(s32[]{:T(128)} %bitcast, (f32[1,4,128,128]{3,2,1,0:T(8,128)}, f32[1,4,128,128]{3,2,1,0:T(8,128)}, s32[1,4,128,128]{3,2,1,0:T(8,128)}, f32[8]{0:T(128)}, s32[4]{0:T(128)}, ...), branch_computations={%region_0.0_spmd, %region_1.0_spmd, %region_2.0_spmd} | conditional | bytes 8 | solution.py:464
  1.3 20.7 %branch_0_fun.1 = (f32[1,4,128,128]{3,2,1,0:T(8,128)S(1)}, f32[1,2,128,128]{3,2,1,0:T(8,128)S(1)}) custom-call(f32[1,4,128,128]{3,2,1,0:T(8,128)} %get-tuple-element.36.source, f32[1,4,128,128]{3,2,1,0:T(8,128)} %get-tuple-element.37.start, s32[1,4,128,128]{3,2,1,0:T(8,128)} %get-tuple-element.38.classes, f32[8]{0:T(128)} %get-tuple-element.39.table_hbm, ...), custom_call_target="tpu_custom_call" | custom-call | tf_op jit(solution)/shard_map/cond/branch_0_fun/pallas_call | solution.py:416
  22.0 0.7 %copy.22 = f32[1,4,128,128]{3,2,1,0:T(8,128)} copy(f32[1,4,128,128]{3,2,1,0:T(8,128)S(1)} %get-tuple-element.70) | data formatting | bytes 524288
  22.7 0.7 %copy.23 = f32[1,2,128,128]{3,2,1,0:T(8,128)} copy(f32[1,2,128,128]{3,2,1,0:T(8,128)S(1)} %get-tuple-element.71) | data formatting | bytes 262144
